TPU v7x, 32 devices: a whole 2x2x4 slice. The times are simulated.
32 devices in a mesh: expert: 8 (over y, x, core), etp: 4 (over z).
Axes of the slice: x: 2, y: 2, z: 4, core: 2. Of those that a mesh axis runs over, the one named last changes fastest.
Arguments:
- tokens: bfloat16 [1024, 2048], P('expert'), may hold values from -6 to 6
- out_grad: bfloat16 [1024, 2048], P('expert'), may hold values from -6 to 6
- routes: int32 [1024, 2], P('expert'), may hold values from 0 to 7, as said below
- combine_weights: float32 [1024, 2], P('expert'), may hold values from 0.2 to 1
- w_gate: bfloat16 [8, 2048, 3584], P('expert', None, 'etp'), may hold values from -0.125 to 0.125
- w_up: bfloat16 [8, 2048, 3584], P('expert', None, 'etp'), may hold values from -0.125 to 0.125
- w_down: bfloat16 [8, 3584, 2048], P('expert', 'etp'), may hold values from -0.09375 to 0.09375
Outputs:
- mixed: bfloat16 [1024, 2048], P('expert')
- tokens_grad: bfloat16 [1024, 2048], P('expert')
- combine_grad: float32 [1024, 2], P('expert')
- gate_weight_grad: bfloat16 [8, 2048, 3584], P('expert', None, 'etp')
- up_weight_grad: bfloat16 [8, 2048, 3584], P('expert', None, 'etp')
- down_weight_grad: bfloat16 [8, 3584, 2048], P('expert', 'etp')
Inputs may be any that keep to these rules, and one draw needn't show every extreme that they name: `routes`: each token names two different experts. No expert is named by more than 32 tokens of one group of 128 consecutive tokens, and one expert, the same in every group, is named by exactly 32 tokens of each group.
All inputs are finite; a program needn't handle non-finite values.
Results may differ from a plain program's by a relative error of at most 0.02.
Values may be sent and summed in bfloat16 or wider, within the bound.
A program may use at most 128 MiB of HBM per device.

v0:
```python
import jax
import jax.numpy as jnp
from jax import lax
from jax.sharding import PartitionSpec as P

TOP = 2


def slot_numbers(routes, expert_count):
    flattened = routes.reshape(-1)
    one_hot = (flattened[:, None] == jnp.arange(expert_count, dtype=jnp.int32)[None, :]).astype(
        jnp.int32
    )
    before = jnp.cumsum(one_hot, axis=0) - one_hot
    return jnp.sum(before * one_hot, axis=1).reshape(routes.shape)


def contract_last(left, right):
    return lax.dot_general(
        left, right, (((1,), (1,)), ((), ())), preferred_element_type=jnp.float32
    )


def contract_first(left, right):
    return lax.dot_general(
        left, right, (((0,), (0,)), ((), ())), preferred_element_type=jnp.float32
    )


def expert_pass(rows_in, rows_grad, gate_w, up_w, down_w):
    gate_pre = jnp.dot(rows_in, gate_w, preferred_element_type=jnp.float32)
    up_pre = jnp.dot(rows_in, up_w, preferred_element_type=jnp.float32)
    gate_sig = jax.nn.sigmoid(gate_pre)
    swish = gate_pre * gate_sig
    hidden = (swish * up_pre).astype(jnp.bfloat16)
    out_part = jnp.dot(hidden, down_w, preferred_element_type=jnp.float32)
    hidden_grad = contract_last(rows_grad, down_w)
    down_grad = contract_first(hidden, rows_grad).astype(jnp.bfloat16)
    gate_grad = (hidden_grad * up_pre * gate_sig * (1.0 + gate_pre * (1.0 - gate_sig))).astype(
        jnp.bfloat16
    )
    up_grad = (hidden_grad * swish).astype(jnp.bfloat16)
    gate_weight_grad = contract_first(rows_in, gate_grad).astype(jnp.bfloat16)
    up_weight_grad = contract_first(rows_in, up_grad).astype(jnp.bfloat16)
    input_part = contract_last(gate_grad, gate_w) + contract_last(up_grad, up_w)
    return (out_part, input_part, gate_weight_grad, up_weight_grad, down_grad)


def shards(tokens, out_grad, routes, combine_weights, w_gate, w_up, w_down):
    expert_count = lax.axis_size("expert")
    token_count, features = tokens.shape
    capacity = token_count // 4
    slots = slot_numbers(routes, expert_count)
    position = routes * capacity + slots
    pair_count = token_count * TOP
    source_index = jnp.full((expert_count * capacity,), pair_count, jnp.int32)
    source_index = source_index.at[position.reshape(-1)].set(
        jnp.arange(pair_count, dtype=jnp.int32)
    )
    zero_row = jnp.zeros((1, features), jnp.bfloat16)
    padded_tokens = jnp.concatenate([tokens, zero_row], axis=0)
    scaled_grad = (combine_weights[:, :, None] * out_grad[:, None, :]).astype(jnp.bfloat16)
    padded_grad = jnp.concatenate([scaled_grad.reshape(pair_count, features), zero_row], axis=0)
    send_rows = padded_tokens[source_index // TOP].reshape(expert_count, capacity, features)
    send_grad = padded_grad[source_index].reshape(expert_count, capacity, features)
    recv_rows, recv_grad = (
        lax.all_to_all(send_rows, "expert", split_axis=0, concat_axis=0, tiled=True),
        lax.all_to_all(send_grad, "expert", split_axis=0, concat_axis=0, tiled=True),
    )
    rows_in = recv_rows.reshape(expert_count * capacity, features)
    rows_grad = recv_grad.reshape(expert_count * capacity, features)
    out_part, input_part, gate_weight_grad, up_weight_grad, down_weight_grad = expert_pass(
        rows_in, rows_grad, w_gate[0], w_up[0], w_down[0]
    )
    out_part = out_part.reshape(expert_count, capacity, features)
    input_part = input_part.reshape(expert_count, capacity, features)
    grad_values = out_grad.astype(jnp.float32)
    out_sum, input_sum = (
        lax.psum(out_part.astype(jnp.bfloat16), "etp").astype(jnp.float32),
        lax.psum(input_part.astype(jnp.bfloat16), "etp").astype(jnp.float32),
    )
    out_back, input_back = (
        lax.all_to_all(
            out_sum.astype(jnp.bfloat16), "expert", split_axis=0, concat_axis=0, tiled=True
        ),
        lax.all_to_all(
            input_sum.astype(jnp.bfloat16), "expert", split_axis=0, concat_axis=0, tiled=True
        ),
    )
    out_pairs = out_back.reshape(expert_count * capacity, features)[position].astype(jnp.float32)
    input_pairs = input_back.reshape(expert_count * capacity, features)[position].astype(
        jnp.float32
    )
    mixed = jnp.sum(combine_weights[:, :, None] * out_pairs, axis=1).astype(jnp.bfloat16)
    combine_grad = jnp.sum(grad_values[:, None, :] * out_pairs, axis=2)
    tokens_grad = jnp.sum(input_pairs, axis=1).astype(jnp.bfloat16)
    return (
        mixed,
        tokens_grad,
        combine_grad,
        gate_weight_grad[None],
        up_weight_grad[None],
        down_weight_grad[None],
    )


def solution(mesh):
    return jax.shard_map(
        shards,
        mesh=mesh,
        in_specs=(
            P("expert", None),
            P("expert", None),
            P("expert", None),
            P("expert", None),
            P("expert", None, "etp"),
            P("expert", None, "etp"),
            P("expert", "etp", None),
        ),
        out_specs=(
            P("expert", None),
            P("expert", None),
            P("expert", None),
            P("expert", None, "etp"),
            P("expert", None, "etp"),
            P("expert", "etp", None),
        ),
        check_vma=False,
    )
```

profile of v0, /device:TPU:0, one launch (start us, length us, event | category | flops | bytes accessed | tf_op | source)
XLA Modules:
  0.0 214.1 jit_solution(2492736653512627251)
XLA Ops:
  7.2 0.8 copy.28
  8.0 0.1 eq.29
  8.1 0.1 eq.25
  8.2 0.6 reduce-window.6
  8.8 0.2 slice_reduce_fusion
  9.1 0.1 fusion.23
  9.2 0.1 reshape.93
  9.3 0.1 copy.30
  9.4 0.7 compare_select_fusion.1
  10.1 0.1 copy.31
  10.2 0.1 reshape.94
  10.4 1.4 scatter_custom_fusion
  11.8 1.1 concatenate.6
  12.9 0.0 copy-start.6
  12.9 0.0 copy-start.2
  12.9 2.3 %gather_fusion = bf16[256,2048]{1,0:T(8,128)(2,1)} fusion(bf16[129,2048]{1,0:T(8,128)(2,1)S(1)} %concatenate.6, s32[1024]{0:T(1024)S(1)} %get-tuple-element.30), kind=kCustom, calls=%fused_computation | custom fusion | bytes 2098176 | tf_op jit(solution)/shard_map/gather | solution.py:64
  15.3 5.2 %all-to-all-start = ((bf16[8,32,2048]{2,1,0:T(8,128)(2,1)}), bf16[8,32,2048]{2,1,0:T(8,128)(2,1)}, u32[]{:S(2)}, u32[]{:S(2)}) async-start(bf16[8,32,2048]{2,1,0:T(8,128)(2,1)} %bitcast.3), calls=%async_computation | async-start | bytes 2097152 | tf_op jit(solution)/shard_map/all_to_all | solution.py:67
  20.4 0.0 copy-done.6
  20.4 0.1 copy.27
  20.5 0.1 mul.69
  20.7 0.0 copy-done.2
  20.7 1.0 mul.71
  21.7 2.4 %mul.72 = f32[256,2048]{1,0:T(8,128)} reshape(f32[128,2,2048]{2,1,0:T(2,128)S(1)} %mul.71) | data formatting | bytes 4194304 | tf_op jit(solution)/shard_map/mul | solution.py:62
  24.2 1.8 multiply_convert_fusion
  26.0 0.1 concatenate.7
  26.1 2.3 %gather_fusion.2 = bf16[256,2048]{1,0:T(8,128)(2,1)} fusion(bf16[257,2048]{1,0:T(8,128)(2,1)S(1)} %concatenate.7, s32[1024]{0:T(1024)S(1)} %get-tuple-element.29), kind=kCustom, calls=%fused_computation.2 | custom fusion | bytes 2098176 | tf_op jit(solution)/shard_map/gather | solution.py:65
  28.4 7.5 %all-to-all-done = bf16[8,32,2048]{2,1,0:T(8,128)(2,1)} async-done(((bf16[8,32,2048]{2,1,0:T(8,128)(2,1)}), bf16[8,32,2048]{2,1,0:T(8,128)(2,1)}, u32[]{:S(2)}, u32[]{:S(2)}) %all-to-all-start) | async-done | bytes 1048608 | tf_op jit(solution)/shard_map/all_to_all | solution.py:67
  35.9 3.6 %all-to-all-start.2 = ((bf16[8,32,2048]{2,1,0:T(8,128)(2,1)}), bf16[8,32,2048]{2,1,0:T(8,128)(2,1)S(1)}, u32[]{:S(2)}, u32[]{:S(2)}) async-start(bf16[8,32,2048]{2,1,0:T(8,128)(2,1)} %bitcast.11), calls=%async_computation.2 | async-start | bytes 2097152 | tf_op jit(solution)/shard_map/all_to_all | solution.py:68
  39.5 0.2 all-reduce.5.cloned.1.call-start
  39.7 4.5 %fusion.6 = f32[256,896]{1,0:T(8,128)} fusion(bf16[256,2048]{1,0:T(8,128)(2,1)} %bitcast.4, bf16[1,2048,896]{2,1,0:T(8,128)(2,1)} %param.12), kind=kOutput, calls=%fused_computation.11 | convolution fusion | flops 939524096 | bytes 5636096 | tf_op jit(solution)/shard_map/dot_general | solution.py:32
  44.3 10.6 %all-to-all-done.2 = bf16[8,32,2048]{2,1,0:T(8,128)(2,1)S(1)} async-done(((bf16[8,32,2048]{2,1,0:T(8,128)(2,1)}), bf16[8,32,2048]{2,1,0:T(8,128)(2,1)S(1)}, u32[]{:S(2)}, u32[]{:S(2)}) %all-to-all-start.2) | async-done | bytes 1048608 | tf_op jit(solution)/shard_map/all_to_all | solution.py:68
  54.9 3.7 %fusion.2 = f32[256,896]{1,0:T(8,128)S(1)} fusion(bf16[256,2048]{1,0:T(8,128)(2,1)S(1)} %bitcast.63, bf16[1,896,2048]{2,1,0:T(8,128)(2,1)} %param.13), kind=kOutput, calls=%fused_computation.7 | convolution fusion | flops 939524096 | bytes 5636096 | tf_op jit(solution)/shard_map/dot_general | solution.py:19
  58.6 0.0 copy-done
  58.6 0.0 copy-done.9
  58.6 0.0 copy-start.7
  58.6 3.0 %multiply_convert_fusion.2 = (bf16[256,896]{1,0:T(8,128)(2,1)S(1)}, bf16[256,896]{1,0:T(8,128)(2,1)S(1)}, bf16[256,896]{1,0:T(8,128)(2,1)S(1)}) fusion(f32[256,896]{1,0:T(8,128)S(1)} %fusion.2, f32[256,896]{1,0:T(8,128)S(1)} %copy-done.9, bf16[256,2048]{1,0:T(8,128)(2,1)} %bitcast.4, bf16[1,2048,896]{2,1,0:T(8,128)(2,1)S(1)} %copy-done), kind=kOutput, calls=%fused_computation.27 | convolution fusion | flops 942964736 | bytes 7929856 | tf_op jit(solution)/shard_map/dot_general | solution.py:31
  61.6 0.0 copy-start.4
  61.7 0.0 copy-start.8
  61.7 0.0 copy-start.1
  61.7 2.3 %fusion.18 = bf16[8,32,2048]{2,1,0:T(8,128)(2,1)} fusion(bf16[8,32,896]{2,1,0:T(8,128)(2,1)S(1)} %bitcast.66, bf16[1,896,2048]{2,1,0:T(8,128)(2,1)S(1)} %copy-done.7), kind=kOutput, calls=%fused_computation.22 | convolution fusion | flops 940048384 | bytes 5177344 | tf_op jit(solution)/shard_map/dot_general | solution.py:36
  64.0 0.3 copy-done.1
  64.3 1.3 fusion.4
  65.6 0.0 copy-done.4
  65.6 0.0 copy-done.8
  65.6 2.3 %fusion.15 = bf16[256,2048]{1,0:T(8,128)(2,1)} fusion(f32[256,2048]{1,0:T(8,128)S(1)} %fusion.4, bf16[256,896]{1,0:T(8,128)(2,1)S(1)} %get-tuple-element.24, bf16[1,2048,896]{2,1,0:T(8,128)(2,1)S(1)} %copy-done), kind=kOutput, calls=%fused_computation.21 | convolution fusion | flops 940572672 | bytes 7274496 | tf_op jit(solution)/shard_map/dot_general | solution.py:19
  67.9 0.0 all-reduce.5.cloned.1.call-update
  67.9 87.0 %all-reduce.5.cloned.1.call-done = (bf16[8,32,2048]{2,1,0:T(8,128)(2,1)}, bf16[8,32,2048]{2,1,0:T(8,128)(2,1)}) async-done(((bf16[8,32,2048]{2,1,0:T(8,128)(2,1)}, bf16[8,32,2048]{2,1,0:T(8,128)(2,1)}), (bf16[8,32,2048]{2,1,0:T(8,128)(2,1)}, bf16[8,32,2048]{2,1,0:T(8,128)(2,1)})) %all-reduce.5.cloned.1.call-update) | async-done | bytes 2097168 | tf_op jit(solution)/shard_map/psum | solution.py:79
  154.9 19.1 %all_to_all.20 = bf16[8,32,2048]{2,1,0:T(8,128)(2,1)S(1)} all-to-all(bf16[8,32,2048]{2,1,0:T(8,128)(2,1)} %get-tuple-element.20), channel_id=1, replica_groups=mesh['expert'=8,'etp'=4] {'expert'}, dimensions={0} | all-to-all | bytes 2097152 | tf_op jit(solution)/shard_map/all_to_all | solution.py:83
  174.0 3.8 %all-to-all-start.3 = ((bf16[8,32,2048]{2,1,0:T(8,128)(2,1)}), bf16[8,32,2048]{2,1,0:T(8,128)(2,1)S(1)}, u32[]{:S(2)}, u32[]{:S(2)}) async-start(bf16[8,32,2048]{2,1,0:T(8,128)(2,1)} %get-tuple-element.21), calls=%async_computation.3 | async-start | bytes 2097152 | tf_op jit(solution)/shard_map/all_to_all | solution.py:86
  177.8 1.1 convert_element_type.61
  178.9 0.1 copy.32
  179.0 0.1 reshape.111
  179.1 4.4 %convert_bitcast_fusion = bf16[1,896,2048]{2,1,0:T(8,128)(2,1)} fusion(bf16[256,896]{1,0:T(8,128)(2,1)} %copy-done.8, bf16[256,2048]{1,0:T(8,128)(2,1)} %bitcast.64), kind=kOutput, calls=%fused_computation.17 | convolution fusion | flops 941359104 | bytes 5177344 | tf_op jit(solution)/shard_map/dot_general | solution.py:25
  183.5 4.4 %convert_bitcast_fusion.2 = bf16[1,2048,896]{2,1,0:T(8,128)(2,1)} fusion(bf16[256,2048]{1,0:T(8,128)(2,1)} %bitcast.4, bf16[256,896]{1,0:T(8,128)(2,1)S(1)} %get-tuple-element.24), kind=kOutput, calls=%fused_computation.19 | convolution fusion | flops 941359104 | bytes 5177344 | tf_op jit(solution)/shard_map/dot_general | solution.py:25
  187.9 0.0 copy-done.5
  187.9 4.4 %convert_bitcast_fusion.1 = bf16[1,2048,896]{2,1,0:T(8,128)(2,1)} fusion(bf16[256,2048]{1,0:T(8,128)(2,1)} %bitcast.4, bf16[256,896]{1,0:T(8,128)(2,1)S(1)} %copy-done.5), kind=kOutput, calls=%fused_computation.18 | convolution fusion | flops 941359104 | bytes 5177344 | tf_op jit(solution)/shard_map/dot_general | solution.py:25
  192.3 1.4 gather_fusion.1
  193.6 0.0 all-to-all-done.3
  193.6 1.4 gather_fusion.3
  195.0 0.7 reshape.130
  195.7 3.6 %reduce_sum.41 = bf16[128,2048]{1,0:T(8,128)(2,1)} reduce(bf16[128,2,2048]{2,1,0:T(2,128)(2,1)S(1)} %reshape.130, bf16[]{:T(256)} %constant.12.clone.1), dimensions={1}, to_apply=%region_7.8 | reduce | flops 262144 | bytes 1572866 | tf_op jit(solution)/shard_map/reduce_sum | solution.py:96
  199.4 1.3 reshape.147
  200.7 6.0 %multiply_reduce_fusion = (f32[128,2]{1,0:T(8,128)S(1)}, bf16[128,2048]{1,0:T(8,128)(2,1)}) fusion(f32[128,2,2048]{2,1,0:T(2,128)S(1)} %reshape.147, f32[128,2048]{1,0:T(8,128)} %convert_element_type.61, f32[128,2]{1,0:T(8,128)S(1)} %copy.27), kind=kLoop, calls=%fused_computation.23 | loop fusion | flops 1834752 | bytes 3672064 | tf_op jit(solution)/shard_map/reduce_sum | solution.py:95
  206.6 0.6 copy.34
  (14 shorter events, 0.1 us)
Async XLA Ops:
  12.9 7.5 %copy-start.6 = (f32[128,2]{0,1:T(2,128)S(1)}, f32[128,2]{0,1:T(2,128)}, u32[]{:S(2)}) copy-start(f32[128,2]{0,1:T(2,128)} %param.10) | copy-start | bytes 3076
  12.9 7.8 %copy-start.2 = (bf16[128,2048]{1,0:T(8,128)(2,1)S(1)}, bf16[128,2048]{1,0:T(8,128)(2,1)}, u32[]{:S(2)}) copy-start(bf16[128,2048]{1,0:T(8,128)(2,1)} %param.8) | copy-start | bytes 1572868
  15.3 20.7 %all-to-all-start = ((bf16[8,32,2048]{2,1,0:T(8,128)(2,1)}), bf16[8,32,2048]{2,1,0:T(8,128)(2,1)}, u32[]{:S(2)}, u32[]{:S(2)}) async-start(bf16[8,32,2048]{2,1,0:T(8,128)(2,1)} %bitcast.3), calls=%async_computation | async-start | bytes 2097152 | tf_op jit(solution)/shard_map/all_to_all | solution.py:67
  35.9 18.9 %all-to-all-start.2 = ((bf16[8,32,2048]{2,1,0:T(8,128)(2,1)}), bf16[8,32,2048]{2,1,0:T(8,128)(2,1)S(1)}, u32[]{:S(2)}, u32[]{:S(2)}) async-start(bf16[8,32,2048]{2,1,0:T(8,128)(2,1)} %bitcast.11), calls=%async_computation.2 | async-start | bytes 2097152 | tf_op jit(solution)/shard_map/all_to_all | solution.py:68
  39.5 115.4 %all-reduce.5.cloned.1.call-start = ((), (), s32[]{:S(2)}) async-start(), calls=%async_computation.4 | async-start | bytes 4194304 | tf_op jit(solution)/shard_map/psum | solution.py:79
  54.9 9.1 %copy-start.3 = (bf16[8,32,2048]{2,1,0:T(8,128)(2,1)}, bf16[8,32,2048]{2,1,0:T(8,128)(2,1)S(1)}, u32[]{:S(2)}) copy-start(bf16[8,32,2048]{2,1,0:T(8,128)(2,1)S(1)} %all-to-all-done.2) | copy-start | bytes 3145732
  54.9 3.8 %copy-start = (bf16[1,2048,896]{2,1,0:T(8,128)(2,1)S(1)}, bf16[1,2048,896]{2,1,0:T(8,128)(2,1)}, u32[]{:S(2)}) copy-start(bf16[1,2048,896]{2,1,0:T(8,128)(2,1)} %param.11) | copy-start | bytes 11010052
  54.9 3.8 %copy-start.9 = (f32[256,896]{1,0:T(8,128)S(1)}, f32[256,896]{1,0:T(8,128)}, u32[]{:S(2)}) copy-start(f32[256,896]{1,0:T(8,128)} %fusion.6) | copy-start | bytes 2752516
  58.6 3.1 %copy-start.7 = (bf16[1,896,2048]{2,1,0:T(8,128)(2,1)S(1)}, bf16[1,896,2048]{2,1,0:T(8,128)(2,1)}, u32[]{:S(2)}) copy-start(bf16[1,896,2048]{2,1,0:T(8,128)(2,1)} %param.13) | copy-start | bytes 11010052
  61.6 3.9 %copy-start.4 = (bf16[256,896]{1,0:T(8,128)(2,1)}, bf16[256,896]{1,0:T(8,128)(2,1)S(1)}, u32[]{:S(2)}) copy-start(bf16[256,896]{1,0:T(8,128)(2,1)S(1)} %get-tuple-element.25) | copy-start | bytes 1376260
  61.7 3.9 %copy-start.8 = (bf16[256,896]{1,0:T(8,128)(2,1)}, bf16[256,896]{1,0:T(8,128)(2,1)S(1)}, u32[]{:S(2)}) copy-start(bf16[256,896]{1,0:T(8,128)(2,1)S(1)} %get-tuple-element.26) | copy-start | bytes 1376260
  61.7 2.6 %copy-start.1 = (bf16[1,2048,896]{2,1,0:T(8,128)(2,1)S(1)}, bf16[1,2048,896]{2,1,0:T(8,128)(2,1)}, u32[]{:S(2)}) copy-start(bf16[1,2048,896]{2,1,0:T(8,128)(2,1)} %param.12) | copy-start | bytes 11010052
  174.0 19.6 %all-to-all-start.3 = ((bf16[8,32,2048]{2,1,0:T(8,128)(2,1)}), bf16[8,32,2048]{2,1,0:T(8,128)(2,1)S(1)}, u32[]{:S(2)}, u32[]{:S(2)}) async-start(bf16[8,32,2048]{2,1,0:T(8,128)(2,1)} %get-tuple-element.21), calls=%async_computation.3 | async-start | bytes 2097152 | tf_op jit(solution)/shard_map/all_to_all | solution.py:86
  183.5 4.4 %copy-start.5 = (bf16[256,896]{1,0:T(8,128)(2,1)S(1)}, bf16[256,896]{1,0:T(8,128)(2,1)}, u32[]{:S(2)}) copy-start(bf16[256,896]{1,0:T(8,128)(2,1)} %copy-done.4) | copy-start | bytes 1376260
Sparse Core Ops, SparseCore 0:
  68.0 86.8 all-reduce.4
where the time goes:
time: 215 us; the launch traced here: 214 us
  waiting for transfers between devices  105 us (49%)
  matrix products  30.2 us (14%)
  blocking collectives  19.1 us (9%)
  local copies, waits for them, and re-layouts  18.8 us (9%)
  between operations  14.3 us (7%)
  other arithmetic  13.9 us (6%)
  starting transfers between devices  12.7 us (6%)
    psum x1, waiting for transfers between devices, shards(): lax.psum(out_part.astype(jnp.bfloat16), 'etp').astype(jnp.float32)  87 us
    all_to_all x1, blocking collectives, shards(): lax.all_to_all(out_sum.astype(jnp.bfloat16), 'expert', split_axis=0, conc...  19.1 us
    dot_general x3, matrix products, contract_first(): lax.dot_general(left, right, (((0,), (0,)), ((), ())), preferred_element_...  13.1 us
    all_to_all x1, waiting for transfers between devices, shards(): lax.all_to_all(send_grad, 'expert', split_axis=0, concat_axis=0, tiled=True)  10.6 us
    all_to_all x1, waiting for transfers between devices, shards(): lax.all_to_all(send_rows, 'expert', split_axis=0, concat_axis=0, tiled=True)  7.53 us
    dot_general x3, matrix products, contract_last(): lax.dot_general(left, right, (((1,), (1,)), ((), ())), preferred_element_...  7.27 us
    reduce_sum x1, other arithmetic, shards(): combine_grad = jnp.sum(grad_values[:, None, :] * out_pairs, axis=2)  5.96 us
    all_to_all x1, starting transfers between devices, shards(): lax.all_to_all(send_rows, 'expert', split_axis=0, concat_axis=0, tiled=True)  5.17 us
  transfers between devices with their start and end apart: 4, of which 3 were waited for; matrix products, arithmetic and copies ran while one was open for 13% of the time, Pallas kernels for 0%

commit v1 on v0

v1 whole, which is shorter than its diff:
```python
import functools

import jax
import jax.numpy as jnp
from jax import lax
from jax.experimental import pallas as pl
from jax.experimental.pallas import tpu as pltpu
from jax.sharding import PartitionSpec as P

MESH = pl.DeviceIdType.MESH
BF16 = jnp.bfloat16
F32 = jnp.float32
CHUNK = 512
LANES = 128


def dot(left, right):
    return jnp.dot(left, right, preferred_element_type=F32)


def contract_last(left, right):
    return lax.dot_general(left, right, (((1,), (1,)), ((), ())), preferred_element_type=F32)


def contract_first(left, right):
    return lax.dot_general(left, right, (((0,), (0,)), ((), ())), preferred_element_type=F32)


def one_hot_places(routes_row, routes_col, cap, places):
    tokens = routes_row.shape[1]
    before_by = lax.broadcasted_iota(jnp.int32, (tokens, tokens), 0)
    before_at = lax.broadcasted_iota(jnp.int32, (tokens, tokens), 1)
    upper = (before_by < before_at).astype(F32).astype(BF16)
    lower = (before_by > before_at).astype(F32).astype(BF16)
    expert_down = lax.broadcasted_iota(jnp.int32, (LANES, tokens), 0)
    expert_across = lax.broadcasted_iota(jnp.int32, (tokens, LANES), 1)
    named_down = [(expert_down == routes_row[k : k + 1, :]).astype(F32) for k in range(2)]
    named_across = [(expert_across == routes_col[:, k : k + 1]).astype(F32) for k in range(2)]
    earlier_down = dot((named_down[0] + named_down[1]).astype(BF16), upper)
    earlier_across = dot(lower, (named_across[0] + named_across[1]).astype(BF16))
    start_down = earlier_down + expert_down.astype(F32) * cap
    start_across = earlier_across + expert_across.astype(F32) * cap
    place_down = lax.broadcasted_iota(jnp.int32, (places, tokens), 0).astype(F32)
    place_across = lax.broadcasted_iota(jnp.int32, (tokens, places), 1).astype(F32)
    scatter, gather = [], []
    for k in range(2):
        row = jnp.sum(named_down[k] * start_down, axis=0, keepdims=True)
        col = jnp.sum(named_across[k] * start_across, axis=1, keepdims=True)
        scatter.append((place_down == row).astype(F32).astype(BF16))
        gather.append((place_across == col).astype(F32).astype(BF16))
    return scatter, gather


def layer_kernel(
    experts,
    lines,
    tokens_ref,
    grad_ref,
    routes_row_ref,
    routes_col_ref,
    weights_ref,
    gate_hbm,
    up_hbm,
    down_hbm,
    mixed_ref,
    tokens_grad_ref,
    combine_ref,
    rows_out,
    rows_grad_out,
    hidden_out,
    gate_grad_out,
    up_grad_out,
    gate_w,
    up_w,
    down_w,
    send,
    rows,
    gate_pre,
    up_pre,
    hidden,
    gate_grad,
    up_grad,
    gather_mat,
    part,
    back,
    line_own,
    line_in,
    line_total,
    dot_own,
    dot_in,
    dot_total,
    load_sem,
    store_sem,
    send_sem,
    recv_sem,
    part_sem,
    back_sem,
    inner_sem,
    line_sem,
    outer_sem,
):
    token_count, features = tokens_ref.shape
    cap = token_count // 4
    places = experts * cap
    chunks = features // CHUNK
    me = lax.axis_index("expert")
    z = lax.axis_index("etp")
    half = lines // 2
    side = 1 - z // half
    inner = z + 2 * side - 1
    outer = z - 2 * side + 1
    has_outer = jnp.logical_and(z > 0, z < lines - 1)
    center = jnp.logical_or(z == half - 1, z == half)
    kind = jnp.where(center, 1, 0)

    loads = [
        pltpu.make_async_copy(src, dst, load_sem.at[i])
        for i, (src, dst) in enumerate(((gate_hbm, gate_w), (up_hbm, up_w), (down_hbm, down_w)))
    ]
    for load in loads:
        load.start()

    barrier = pltpu.get_barrier_semaphore()

    def greet(d, carry):
        peer = lax.rem(me + d, experts)
        pl.semaphore_signal(barrier, inc=1, device_id={"expert": peer}, device_id_type=MESH)
        return carry

    lax.fori_loop(1, experts, greet, 0)
    pl.semaphore_signal(barrier, inc=1, device_id={"etp": inner}, device_id_type=MESH)

    @pl.when(has_outer)
    def _():
        pl.semaphore_signal(barrier, inc=1, device_id={"etp": outer}, device_id_type=MESH)

    def block_of(index):
        return pl.ds(pl.multiple_of(index * cap, cap), cap)

    mine = block_of(me)

    def dispatch(i, peer, owner):
        return pltpu.make_async_remote_copy(
            src_ref=send.at[i, block_of(peer)],
            dst_ref=rows.at[i, block_of(owner)],
            send_sem=send_sem.at[i, peer],
            recv_sem=recv_sem.at[i, owner],
            device_id={"expert": peer},
            device_id_type=MESH,
        )

    def give_back(i, peer, owner):
        return pltpu.make_async_remote_copy(
            src_ref=part.at[i, block_of(peer)],
            dst_ref=back.at[i, block_of(owner)],
            send_sem=part_sem.at[i, peer],
            recv_sem=back_sem.at[i, owner],
            device_id={"expert": peer},
            device_id_type=MESH,
        )

    def each_peer(action):
        def body(d, carry):
            action(lax.rem(me + d, experts))
            return carry

        lax.fori_loop(1, experts, body, 0)

    scatter, gather = one_hot_places(routes_row_ref[...], routes_col_ref[...], cap, places)
    for k in range(2):
        gather_mat[k] = gather[k]
    scatter_both = scatter[0] + scatter[1]
    for c in range(chunks):
        cols = slice(c * CHUNK, (c + 1) * CHUNK)
        send[0, :, cols] = dot(scatter_both, tokens_ref[:, cols]).astype(BF16)

    pl.semaphore_wait(barrier, experts + jnp.where(has_outer, 1, 0))
    each_peer(lambda q: dispatch(0, q, me).start())
    rows[0, mine] = send[0, mine]
    for c in range(chunks):
        cols = slice(c * CHUNK, (c + 1) * CHUNK)
        value = grad_ref[:, cols].astype(F32)
        scaled = [(weights_ref[:, k : k + 1] * value).astype(BF16) for k in range(2)]
        send[1, :, cols] = (dot(scatter[0], scaled[0]) + dot(scatter[1], scaled[1])).astype(BF16)
    each_peer(lambda q: dispatch(1, q, me).start())
    rows[1, mine] = send[1, mine]

    loads[0].wait()
    loads[1].wait()
    loads[2].wait()
    each_peer(lambda q: dispatch(0, me, q).wait_recv())
    gate_pre[...] = dot(rows[0], gate_w[...])
    up_pre[...] = dot(rows[0], up_w[...])
    gate_value = gate_pre[...]
    hidden[...] = (gate_value * jax.nn.sigmoid(gate_value) * up_pre[...]).astype(BF16)
    for c in range(chunks):
        part[c] = dot(hidden[...], down_w[:, c * CHUNK : (c + 1) * CHUNK]).astype(BF16)
        each_peer(lambda q, c=c: give_back(c, q, me).start())
        back[c, mine] = part[c, mine]

    each_peer(lambda q: dispatch(1, me, q).wait_recv())
    hidden_grad = contract_last(rows[1], down_w[...])
    gate_value = gate_pre[...]
    sig = jax.nn.sigmoid(gate_value)
    gate_grad[...] = (
        hidden_grad * up_pre[...] * sig * (1.0 + gate_value * (1.0 - sig))
    ).astype(BF16)
    up_grad[...] = (hidden_grad * (gate_value * sig)).astype(BF16)
    for c in range(chunks):
        i = chunks + c
        rows_of = slice(c * CHUNK, (c + 1) * CHUNK)
        part[i] = (
            contract_last(gate_grad[...], gate_w[rows_of, :])
            + contract_last(up_grad[...], up_w[rows_of, :])
        ).astype(BF16)
        each_peer(lambda q, i=i: give_back(i, q, me).start())
        back[i, mine] = part[i, mine]

    stores = [
        pltpu.make_async_copy(src, dst, store_sem.at[i])
        for i, (src, dst) in enumerate(
            (
                (rows.at[0], rows_out),
                (rows.at[1], rows_grad_out),
                (hidden, hidden_out),
                (gate_grad, gate_grad_out),
                (up_grad, up_grad_out),
            )
        )
    ]
    for store in stores:
        store.start()

    last = 2 * chunks

    def line_refs(i):
        if i == last:
            return dot_own, dot_in.at[0], dot_in.at[1], dot_total
        return line_own.at[i], line_in.at[0, i], line_in.at[1, i], line_total.at[i]

    def to_inner(i):
        own = line_refs(i)[0]
        target = dot_in.at[kind] if i == last else line_in.at[kind, i]
        return pltpu.make_async_remote_copy(
            src_ref=own,
            dst_ref=target,
            send_sem=inner_sem.at[i],
            recv_sem=line_sem.at[kind, i],
            device_id={"etp": inner},
            device_id_type=MESH,
        )

    def to_outer(i):
        _, _, target, total = line_refs(i)
        return pltpu.make_async_remote_copy(
            src_ref=total,
            dst_ref=target,
            send_sem=outer_sem.at[i],
            recv_sem=line_sem.at[1, i],
            device_id={"etp": outer},
            device_id_type=MESH,
        )

    def arrived(i, which):
        own, _, _, _ = line_refs(i)
        target = line_refs(i)[1 + which]
        return pltpu.make_async_remote_copy(
            src_ref=own,
            dst_ref=target,
            send_sem=inner_sem.at[i],
            recv_sem=line_sem.at[which, i],
            device_id={"etp": inner},
            device_id_type=MESH,
        )

    def inward(i, value):
        own, from_outer, _, _ = line_refs(i)

        @pl.when(has_outer)
        def _():
            arrived(i, 0).wait_recv()
            own[...] = (value + from_outer[...].astype(F32)).astype(own.dtype)

        @pl.when(jnp.logical_not(has_outer))
        def _():
            own[...] = value.astype(own.dtype)

        to_inner(i).start()

    def outward(i):
        own, _, from_inner, total = line_refs(i)
        arrived(i, 1).wait_recv()

        @pl.when(center)
        def _():
            total[...] = (own[...].astype(F32) + from_inner[...].astype(F32)).astype(own.dtype)

        @pl.when(jnp.logical_not(center))
        def _():
            total[...] = from_inner[...]

        @pl.when(has_outer)
        def _():
            to_outer(i).start()

        if i < chunks:
            mixed_ref[:, i * CHUNK : (i + 1) * CHUNK] = total[...]
        elif i < last:
            c = i - chunks
            tokens_grad_ref[:, c * CHUNK : (c + 1) * CHUNK] = total[...]
        else:
            combine_ref[...] = total[...]

    order = list(range(chunks)) + [last] + list(range(chunks, last))
    weight = [weights_ref[:, k : k + 1] for k in range(2)]
    products = [None, None]
    waiting = []
    for i in order:
        if i == last:
            sums = [jnp.sum(product, axis=1, keepdims=True) for product in products]
            lane = lax.broadcasted_iota(jnp.int32, (token_count, LANES), 1)
            table = jnp.where(lane == 0, sums[0], jnp.where(lane == 1, sums[1], 0.0))
            inward(i, table.T[:8])
        else:
            each_peer(lambda q, i=i: give_back(i, me, q).wait_recv())
            if i < chunks:
                pairs = [dot(gather_mat[k], back[i]) for k in range(2)]
                value = grad_ref[:, i * CHUNK : (i + 1) * CHUNK].astype(F32)
                for k in range(2):
                    term = value * pairs[k]
                    for s in range(CHUNK // LANES):
                        piece = term[:, s * LANES : (s + 1) * LANES]
                        products[k] = piece if products[k] is None else products[k] + piece
                inward(i, weight[0] * pairs[0] + weight[1] * pairs[1])
            else:
                inward(i, dot(gather_mat[0] + gather_mat[1], back[i]))
        waiting.append(i)
        if len(waiting) > 2:
            outward(waiting.pop(0))
    for i in waiting:
        outward(i)

    for store in stores:
        store.wait()
    each_peer(lambda q: dispatch(0, q, me).wait_send())
    each_peer(lambda q: dispatch(1, q, me).wait_send())
    for i in range(last):
        each_peer(lambda q, i=i: give_back(i, q, me).wait_send())
    for i in range(last + 1):
        to_inner(i).wait_send()

    @pl.when(has_outer)
    def _():
        for i in range(last + 1):
            to_outer(i).wait_send()


def weight_grad_kernel(
    rows_ref, rows_grad_ref, hidden_ref, gate_ref, up_ref, gate_out, up_out, down_out, turned
):
    @pl.when(pl.program_id(0) == 0)
    def _():
        turned[...] = hidden_ref[...].T

    rows_t = rows_ref[...].T
    gate_out[...] = dot(rows_t, gate_ref[...]).astype(BF16)
    up_out[...] = dot(rows_t, up_ref[...]).astype(BF16)
    down_out[...] = dot(turned[...], rows_grad_ref[...]).astype(BF16)


def weight_grads(rows, rows_grad, hidden, gate_grad, up_grad):
    places, features = rows.shape
    units = hidden.shape[1]
    block = 256
    by_feature = pl.BlockSpec((places, block), lambda i: (0, i))
    whole = pl.BlockSpec((places, units), lambda i: (0, 0))
    tall = pl.BlockSpec((block, units), lambda i: (i, 0))
    wide = pl.BlockSpec((units, block), lambda i: (0, i))
    return pl.pallas_call(
        weight_grad_kernel,
        grid=(features // block,),
        in_specs=[by_feature, by_feature, whole, whole, whole],
        out_specs=[tall, tall, wide],
        out_shape=[
            jax.ShapeDtypeStruct((features, units), BF16),
            jax.ShapeDtypeStruct((features, units), BF16),
            jax.ShapeDtypeStruct((units, features), BF16),
        ],
        scratch_shapes=[pltpu.VMEM((units, places), BF16)],
        compiler_params=pltpu.CompilerParams(vmem_limit_bytes=32 << 20),
        cost_estimate=pl.CostEstimate(
            flops=6 * places * features * units,
            bytes_accessed=6 * features * units + 4 * places * features + 6 * places * units,
            transcendentals=0,
        ),
    )(rows, rows_grad, hidden, gate_grad, up_grad)


def shards(experts, lines, tokens, out_grad, routes, combine_weights, w_gate, w_up, w_down):
    token_count, features = tokens.shape
    units = w_gate.shape[2]
    cap = token_count // 4
    places = experts * cap
    chunks = features // CHUNK
    vmem = pl.BlockSpec(memory_space=pltpu.VMEM)
    hbm = pl.BlockSpec(memory_space=pl.ANY)
    dma = pltpu.SemaphoreType.DMA
    outs = pl.pallas_call(
        functools.partial(layer_kernel, experts, lines),
        in_specs=[vmem] * 5 + [hbm] * 3,
        out_specs=[vmem] * 3 + [hbm] * 5,
        out_shape=[
            jax.ShapeDtypeStruct((token_count, features), BF16),
            jax.ShapeDtypeStruct((token_count, features), BF16),
            jax.ShapeDtypeStruct((8, token_count), F32),
            jax.ShapeDtypeStruct((places, features), BF16),
            jax.ShapeDtypeStruct((places, features), BF16),
            jax.ShapeDtypeStruct((places, units), BF16),
            jax.ShapeDtypeStruct((places, units), BF16),
            jax.ShapeDtypeStruct((places, units), BF16),
        ],
        scratch_shapes=[
            pltpu.VMEM((features, units), BF16),
            pltpu.VMEM((features, units), BF16),
            pltpu.VMEM((units, features), BF16),
            pltpu.VMEM((2, places, features), BF16),
            pltpu.VMEM((2, places, features), BF16),
            pltpu.VMEM((places, units), F32),
            pltpu.VMEM((places, units), F32),
            pltpu.VMEM((places, units), BF16),
            pltpu.VMEM((places, units), BF16),
            pltpu.VMEM((places, units), BF16),
            pltpu.VMEM((2, token_count, places), BF16),
            pltpu.VMEM((2 * chunks, places, CHUNK), BF16),
            pltpu.VMEM((2 * chunks, places, CHUNK), BF16),
            pltpu.VMEM((2 * chunks, token_count, CHUNK), BF16),
            pltpu.VMEM((2, 2 * chunks, token_count, CHUNK), BF16),
            pltpu.VMEM((2 * chunks, token_count, CHUNK), BF16),
            pltpu.VMEM((8, token_count), F32),
            pltpu.VMEM((2, 8, token_count), F32),
            pltpu.VMEM((8, token_count), F32),
            dma((3,)),
            dma((5,)),
            dma((2, experts)),
            dma((2, experts)),
            dma((2 * chunks, experts)),
            dma((2 * chunks, experts)),
            dma((2 * chunks + 1,)),
            dma((2, 2 * chunks + 1)),
            dma((2 * chunks + 1,)),
        ],
        compiler_params=pltpu.CompilerParams(
            collective_id=0, has_side_effects=True, vmem_limit_bytes=56 << 20
        ),
        cost_estimate=pl.CostEstimate(
            flops=12 * places * features * units,
            bytes_accessed=6 * features * units,
            transcendentals=2 * places * units,
        ),
    )(tokens, out_grad, routes.T, routes, combine_weights, w_gate[0], w_up[0], w_down[0])
    mixed, tokens_grad, combine, rows, rows_grad, hidden, gate_grad, up_grad = outs
    gate_wg, up_wg, down_wg = weight_grads(rows, rows_grad, hidden, gate_grad, up_grad)
    return mixed, tokens_grad, combine[:2].T, gate_wg[None], up_wg[None], down_wg[None]


def solution(mesh):
    rows = P("expert", None)
    columns = P("expert", None, "etp")
    return jax.shard_map(
        functools.partial(shards, mesh.shape["expert"], mesh.shape["etp"]),
        mesh=mesh,
        in_specs=(rows, rows, rows, rows, columns, columns, P("expert", "etp", None)),
        out_specs=(rows, rows, rows, columns, columns, P("expert", "etp", None)),
        check_vma=False,
    )
```

time: 215 us -> 129 us (0.60)
  Pallas kernels: 0 us -> 116 us
  waiting for transfers between devices: 105 us -> 0 us
  matrix products: 30.2 us -> 0 us
  blocking collectives: 19.1 us -> 0 us
  other arithmetic: 13.9 us -> 0 us
  between operations: 14.3 us -> 0.65 us
  starting transfers between devices: 12.7 us -> 0 us
  local copies, waits for them, and re-layouts: 18.8 us -> 11.2 us
    pallas_call x0 -> x2, Pallas kernels: none -> 116 us  [the longest x1 109 us: shards(): pl.pallas_call(functools.partial(layer_kernel, experts, lines), in_specs=...]
    psum x1 -> x0, waiting for transfers between devices: 87 us -> none  [shards(): lax.psum(out_part.astype(jnp.bfloat16), 'etp').astype(jnp.float32)]
    dot_general x9 -> x0, matrix products: 30.2 us -> none  [the longest x3 13.1 us: contract_first(): lax.dot_general(left, right, (((0,), (0,)), ((), ())), preferred_element_...]
    all_to_all x1 -> x0, blocking collectives: 19.1 us -> none  [shards(): lax.all_to_all(out_sum.astype(jnp.bfloat16), 'expert', split_axis=0, conc...]
    all_to_all x3 -> x0, waiting for transfers between devices: 18.1 us -> none  [the longest x1 10.6 us: shards(): lax.all_to_all(send_grad, 'expert', split_axis=0, concat_axis=0, tiled=True)]
    all_to_all x3 -> x0, starting transfers between devices: 12.5 us -> none  [the longest x1 5.17 us: shards(): lax.all_to_all(send_rows, 'expert', split_axis=0, concat_axis=0, tiled=True)]
    reduce_sum x3 -> x0, other arithmetic: 9.69 us -> none  [the longest x1 5.96 us: shards(): combine_grad = jnp.sum(grad_values[:, None, :] * out_pairs, axis=2)]
    gather x5 -> x0, local copies, waits for them, and re-layouts: 8.09 us -> none  [the longest x1 2.33 us: shards(): padded_grad[source_index].reshape(expert_count, capacity, features)]
  transfers between devices with their start and end apart: 4 -> 0, of which waited for: 3 -> 0; matrix products, arithmetic and copies ran while one was open for 13% -> 0% of each run, Pallas kernels for 0% -> 0%
where the time goes in v1:
time: 129 us; the launch traced here: 128 us
  Pallas kernels  116 us (90%)
  local copies, waits for them, and re-layouts  11.2 us (9%)
    pallas_call x1, Pallas kernels, shards(): pl.pallas_call(functools.partial(layer_kernel, experts, lines), in_specs=...  109 us
    unnamed x18, local copies, waits for them, and re-layouts  9.92 us
    pallas_call x1, Pallas kernels, weight_grads(): pl.pallas_call(weight_grad_kernel, grid=(features // block,), in_specs=[b...  7.08 us

profile of v1, /device:TPU:0, one launch (start us, length us, event | category | flops | bytes accessed | tf_op | source)
XLA Modules:
  0.0 128.1 jit_solution(2172846274739481766)
XLA Ops:
  0.6 1.4 %copy.14.weights_ref = f32[128,2]{1,0:T(8,128)} copy(f32[128,2]{0,1:T(2,128)} %param.10) | data formatting | bytes 2048 | tf_op args[3]
  2.0 1.4 %copy.13.routes_col_ref = s32[128,2]{1,0:T(8,128)} copy(s32[128,2]{0,1:T(2,128)} %param.9) | data formatting | bytes 2048 | tf_op args[2]
  3.5 109.2 %shard_map.118 = (bf16[128,2048]{1,0:T(8,128)(2,1)}, bf16[128,2048]{1,0:T(8,128)(2,1)}, f32[8,128]{1,0:T(8,128)}, bf16[256,2048]{1,0:T(8,128)(2,1)}, bf16[256,20...) custom-call(bf16[128,2048]{1,0:T(8,128)(2,1)} %tokens_ref.1, ...), custom_call_target="tpu_custom_call" | custom-call | flops 5637144576 | bytes 11010048 | tf_op jit(solution)/shard_map/pallas_call | solution.py:408
  112.7 1.2 slice_bitcast_fusion
  114.0 0.0 copy-start
  114.0 1.2 copy-done
  115.2 0.0 copy-start.1
  115.2 1.2 copy-done.1
  116.4 0.0 copy-start.2
  116.4 1.0 copy-done.2
  117.4 0.0 copy-start.3
  117.4 1.0 copy-done.3
  118.5 0.0 copy-start.4
  118.5 1.0 copy-done.4
  119.5 0.0 copy-start.6
  119.5 0.0 copy-start.5
  119.5 7.1 %shard_map.119 = (bf16[2048,896]{1,0:T(8,128)(2,1)}, bf16[2048,896]{1,0:T(8,128)(2,1)}, bf16[896,2048]{1,0:T(8,128)(2,1)}) custom-call(bf16[256,2048]{1,0:T(8,128)(2,1)S(1)} %copy-done, bf16[256,2048]{1,0:T(8,128)(2,1)S(1)} %copy-done.1, bf16[256,896]{1,0:T(8,128)(2,1)S(1)} %copy-done.2, bf16[256,896]{1,0:T(8,128)(2,1)S(1)} %copy-done.3, ...), custom_call_target="tpu_custom_call" | custom-call | flops 2818572288 | bytes 14483456 | tf_op jit(solution)/shard_map/pallas_call | solution.py:379
  126.6 0.0 copy-done.6
  126.6 0.8 copy.17
  127.4 0.0 copy-done.5
  127.4 0.8 copy.18
Async XLA Ops:
  114.0 1.2 copy-start
  115.2 1.2 copy-start.1
  116.4 1.0 copy-start.2
  117.4 1.0 copy-start.3
  118.5 1.0 copy-start.4
  119.5 7.1 %copy-start.6 = (bf16[128,2048]{1,0:T(8,128)(2,1)S(1)}, bf16[128,2048]{1,0:T(8,128)(2,1)}, u32[]{:S(2)}) copy-start(bf16[128,2048]{1,0:T(8,128)(2,1)} %get-tuple-element.34) | copy-start | bytes 1572868
  119.5 7.9 %copy-start.5 = (bf16[128,2048]{1,0:T(8,128)(2,1)S(1)}, bf16[128,2048]{1,0:T(8,128)(2,1)}, u32[]{:S(2)}) copy-start(bf16[128,2048]{1,0:T(8,128)(2,1)} %get-tuple-element.35) | copy-start | bytes 1572868

commit v2 on v1

--- a/solution.py
+++ b/solution.py
@@ -10,8 +10,9 @@
 MESH = pl.DeviceIdType.MESH
 BF16 = jnp.bfloat16
 F32 = jnp.float32
-CHUNK = 512
+CHUNK = 256
 LANES = 128
+LAG = 2
 
 
 def dot(left, right):
@@ -35,7 +36,9 @@
     expert_down = lax.broadcasted_iota(jnp.int32, (LANES, tokens), 0)
     expert_across = lax.broadcasted_iota(jnp.int32, (tokens, LANES), 1)
     named_down = [(expert_down == routes_row[k : k + 1, :]).astype(F32) for k in range(2)]
-    named_across = [(expert_across == routes_col[:, k : k + 1]).astype(F32) for k in range(2)]
+    named_across = [
+        (expert_across.astype(F32) == routes_col[:, k : k + 1]).astype(F32) for k in range(2)
+    ]
     earlier_down = dot((named_down[0] + named_down[1]).astype(BF16), upper)
     earlier_across = dot(lower, (named_across[0] + named_across[1]).astype(BF16))
     start_down = earlier_down + expert_down.astype(F32) * cap
@@ -56,8 +59,7 @@
     lines,
     tokens_ref,
     grad_ref,
-    routes_row_ref,
-    routes_col_ref,
+    routes_ref,
     weights_ref,
     gate_hbm,
     up_hbm,
@@ -65,9 +67,9 @@
     mixed_ref,
     tokens_grad_ref,
     combine_ref,
-    rows_out,
+    rows_t_out,
     rows_grad_out,
-    hidden_out,
+    hidden_t_out,
     gate_grad_out,
     up_grad_out,
     gate_w,
@@ -80,6 +82,8 @@
     hidden,
     gate_grad,
     up_grad,
+    rows_t,
+    hidden_t,
     gather_mat,
     part,
     back,
@@ -166,7 +170,12 @@
 
         lax.fori_loop(1, experts, body, 0)
 
-    scatter, gather = one_hot_places(routes_row_ref[...], routes_col_ref[...], cap, places)
+    sub = lax.broadcasted_iota(jnp.int32, (LANES, token_count), 0)
+    table = jnp.where(sub == 0, routes_ref[0:1, :], routes_ref[1:2, :]).astype(F32)
+    table = jnp.where(sub == 2, weights_ref[0:1, :], table)
+    table = jnp.where(sub == 3, weights_ref[1:2, :], table).T
+    weight = [table[:, 2 + k : 3 + k] for k in range(2)]
+    scatter, gather = one_hot_places(routes_ref[...], table, cap, places)
     for k in range(2):
         gather_mat[k] = gather[k]
     scatter_both = scatter[0] + scatter[1]
@@ -180,7 +189,7 @@
     for c in range(chunks):
         cols = slice(c * CHUNK, (c + 1) * CHUNK)
         value = grad_ref[:, cols].astype(F32)
-        scaled = [(weights_ref[:, k : k + 1] * value).astype(BF16) for k in range(2)]
+        scaled = [(weight[k] * value).astype(BF16) for k in range(2)]
         send[1, :, cols] = (dot(scatter[0], scaled[0]) + dot(scatter[1], scaled[1])).astype(BF16)
     each_peer(lambda q: dispatch(1, q, me).start())
     rows[1, mine] = send[1, mine]
@@ -198,6 +207,11 @@
         each_peer(lambda q, c=c: give_back(c, q, me).start())
         back[c, mine] = part[c, mine]
 
+    hidden_t[...] = hidden[...].T
+    for c in range(chunks):
+        cols = slice(c * CHUNK, (c + 1) * CHUNK)
+        rows_t[cols, :] = rows[0, :, cols].T
+
     each_peer(lambda q: dispatch(1, me, q).wait_recv())
     hidden_grad = contract_last(rows[1], down_w[...])
     gate_value = gate_pre[...]
@@ -206,23 +220,13 @@
         hidden_grad * up_pre[...] * sig * (1.0 + gate_value * (1.0 - sig))
     ).astype(BF16)
     up_grad[...] = (hidden_grad * (gate_value * sig)).astype(BF16)
-    for c in range(chunks):
-        i = chunks + c
-        rows_of = slice(c * CHUNK, (c + 1) * CHUNK)
-        part[i] = (
-            contract_last(gate_grad[...], gate_w[rows_of, :])
-            + contract_last(up_grad[...], up_w[rows_of, :])
-        ).astype(BF16)
-        each_peer(lambda q, i=i: give_back(i, q, me).start())
-        back[i, mine] = part[i, mine]
-
     stores = [
         pltpu.make_async_copy(src, dst, store_sem.at[i])
         for i, (src, dst) in enumerate(
             (
-                (rows.at[0], rows_out),
+                (rows_t, rows_t_out),
                 (rows.at[1], rows_grad_out),
-                (hidden, hidden_out),
+                (hidden_t, hidden_t_out),
                 (gate_grad, gate_grad_out),
                 (up_grad, up_grad_out),
             )
@@ -309,34 +313,39 @@
             c = i - chunks
             tokens_grad_ref[:, c * CHUNK : (c + 1) * CHUNK] = total[...]
         else:
-            combine_ref[...] = total[...]
-
-    order = list(range(chunks)) + [last] + list(range(chunks, last))
-    weight = [weights_ref[:, k : k + 1] for k in range(2)]
+            combine_ref[...] = total[:2]
+
     products = [None, None]
-    waiting = []
-    for i in order:
-        if i == last:
-            sums = [jnp.sum(product, axis=1, keepdims=True) for product in products]
-            lane = lax.broadcasted_iota(jnp.int32, (token_count, LANES), 1)
-            table = jnp.where(lane == 0, sums[0], jnp.where(lane == 1, sums[1], 0.0))
-            inward(i, table.T[:8])
-        else:
-            each_peer(lambda q, i=i: give_back(i, me, q).wait_recv())
-            if i < chunks:
-                pairs = [dot(gather_mat[k], back[i]) for k in range(2)]
-                value = grad_ref[:, i * CHUNK : (i + 1) * CHUNK].astype(F32)
-                for k in range(2):
-                    term = value * pairs[k]
-                    for s in range(CHUNK // LANES):
-                        piece = term[:, s * LANES : (s + 1) * LANES]
-                        products[k] = piece if products[k] is None else products[k] + piece
-                inward(i, weight[0] * pairs[0] + weight[1] * pairs[1])
-            else:
-                inward(i, dot(gather_mat[0] + gather_mat[1], back[i]))
-        waiting.append(i)
-        if len(waiting) > 2:
-            outward(waiting.pop(0))
+    for i in range(chunks):
+        j = chunks + i
+        rows_of = slice(i * CHUNK, (i + 1) * CHUNK)
+        part[j] = (
+            contract_last(gate_grad[...], gate_w[rows_of, :])
+            + contract_last(up_grad[...], up_w[rows_of, :])
+        ).astype(BF16)
+        each_peer(lambda q, j=j: give_back(j, q, me).start())
+        back[j, mine] = part[j, mine]
+        each_peer(lambda q, i=i: give_back(i, me, q).wait_recv())
+        pairs = [dot(gather_mat[k], back[i]) for k in range(2)]
+        value = grad_ref[:, rows_of].astype(F32)
+        for k in range(2):
+            term = value * pairs[k]
+            for s in range(CHUNK // LANES):
+                piece = term[:, s * LANES : (s + 1) * LANES]
+                products[k] = piece if products[k] is None else products[k] + piece
+        inward(i, weight[0] * pairs[0] + weight[1] * pairs[1])
+        if i >= LAG:
+            outward(i - LAG)
+    sums = [jnp.sum(product, axis=1, keepdims=True) for product in products]
+    lane = lax.broadcasted_iota(jnp.int32, (token_count, LANES), 1)
+    inward(last, jnp.where(lane == 0, sums[0], jnp.where(lane == 1, sums[1], 0.0)).T[:8])
+    waiting = list(range(chunks - LAG, chunks)) + [last]
+    gather_both = gather_mat[0] + gather_mat[1]
+    for j in range(chunks, last):
+        outward(waiting.pop(0))
+        each_peer(lambda q, j=j: give_back(j, me, q).wait_recv())
+        inward(j, dot(gather_both, back[j]))
+        waiting.append(j)
     for i in waiting:
         outward(i)
 
@@ -356,44 +365,68 @@
 
 
 def weight_grad_kernel(
-    rows_ref, rows_grad_ref, hidden_ref, gate_ref, up_ref, gate_out, up_out, down_out, turned
+    rows_t_ref,
+    rows_grad_ref,
+    hidden_t_ref,
+    gate_ref,
+    up_ref,
+    mixed_ref,
+    tokens_grad_ref,
+    combine_ref,
+    gate_out,
+    up_out,
+    down_out,
+    mixed_out,
+    tokens_grad_out,
+    combine_out,
 ):
-    @pl.when(pl.program_id(0) == 0)
-    def _():
-        turned[...] = hidden_ref[...].T
-
-    rows_t = rows_ref[...].T
-    gate_out[...] = dot(rows_t, gate_ref[...]).astype(BF16)
-    up_out[...] = dot(rows_t, up_ref[...]).astype(BF16)
-    down_out[...] = dot(turned[...], rows_grad_ref[...]).astype(BF16)
-
-
-def weight_grads(rows, rows_grad, hidden, gate_grad, up_grad):
-    places, features = rows.shape
-    units = hidden.shape[1]
+    mixed_out[...] = mixed_ref[...]
+    tokens_grad_out[...] = tokens_grad_ref[...]
+    combine_out[...] = combine_ref[...]
+    gate_out[...] = dot(rows_t_ref[...], gate_ref[...]).astype(BF16)
+    up_out[...] = dot(rows_t_ref[...], up_ref[...]).astype(BF16)
+    down_out[...] = dot(hidden_t_ref[...], rows_grad_ref[...]).astype(BF16)
+
+
+def weight_grads(rows_t, rows_grad, hidden_t, gate_grad, up_grad, mixed, tokens_grad, combine):
+    places, features = rows_grad.shape
+    units = gate_grad.shape[1]
     block = 256
-    by_feature = pl.BlockSpec((places, block), lambda i: (0, i))
-    whole = pl.BlockSpec((places, units), lambda i: (0, 0))
     tall = pl.BlockSpec((block, units), lambda i: (i, 0))
     wide = pl.BlockSpec((units, block), lambda i: (0, i))
+    whole = pl.BlockSpec((places, units), lambda i: (0, 0))
+    token_count = mixed.shape[0]
+    token_cols = pl.BlockSpec((token_count, block), lambda i: (0, i))
+    pair_sums = pl.BlockSpec((2, token_count), lambda i: (0, 0))
     return pl.pallas_call(
         weight_grad_kernel,
         grid=(features // block,),
-        in_specs=[by_feature, by_feature, whole, whole, whole],
-        out_specs=[tall, tall, wide],
+        in_specs=[
+            pl.BlockSpec((block, places), lambda i: (i, 0)),
+            pl.BlockSpec((places, block), lambda i: (0, i)),
+            pl.BlockSpec((units, places), lambda i: (0, 0)),
+            whole,
+            whole,
+            token_cols,
+            token_cols,
+            pair_sums,
+        ],
+        out_specs=[tall, tall, wide, token_cols, token_cols, pair_sums],
         out_shape=[
             jax.ShapeDtypeStruct((features, units), BF16),
             jax.ShapeDtypeStruct((features, units), BF16),
             jax.ShapeDtypeStruct((units, features), BF16),
+            jax.ShapeDtypeStruct((token_count, features), BF16),
+            jax.ShapeDtypeStruct((token_count, features), BF16),
+            jax.ShapeDtypeStruct((2, token_count), F32),
         ],
-        scratch_shapes=[pltpu.VMEM((units, places), BF16)],
-        compiler_params=pltpu.CompilerParams(vmem_limit_bytes=32 << 20),
+        compiler_params=pltpu.CompilerParams(vmem_limit_bytes=60 << 20),
         cost_estimate=pl.CostEstimate(
             flops=6 * places * features * units,
             bytes_accessed=6 * features * units + 4 * places * features + 6 * places * units,
             transcendentals=0,
         ),
-    )(rows, rows_grad, hidden, gate_grad, up_grad)
+    )(rows_t, rows_grad, hidden_t, gate_grad, up_grad, mixed, tokens_grad, combine)
 
 
 def shards(experts, lines, tokens, out_grad, routes, combine_weights, w_gate, w_up, w_down):
@@ -407,15 +440,15 @@
     dma = pltpu.SemaphoreType.DMA
     outs = pl.pallas_call(
         functools.partial(layer_kernel, experts, lines),
-        in_specs=[vmem] * 5 + [hbm] * 3,
+        in_specs=[vmem] * 4 + [hbm] * 3,
         out_specs=[vmem] * 3 + [hbm] * 5,
         out_shape=[
             jax.ShapeDtypeStruct((token_count, features), BF16),
             jax.ShapeDtypeStruct((token_count, features), BF16),
-            jax.ShapeDtypeStruct((8, token_count), F32),
+            jax.ShapeDtypeStruct((2, token_count), F32),
+            jax.ShapeDtypeStruct((features, places), BF16),
             jax.ShapeDtypeStruct((places, features), BF16),
-            jax.ShapeDtypeStruct((places, features), BF16),
-            jax.ShapeDtypeStruct((places, units), BF16),
+            jax.ShapeDtypeStruct((units, places), BF16),
             jax.ShapeDtypeStruct((places, units), BF16),
             jax.ShapeDtypeStruct((places, units), BF16),
         ],
@@ -430,6 +463,8 @@
             pltpu.VMEM((places, units), BF16),
             pltpu.VMEM((places, units), BF16),
             pltpu.VMEM((places, units), BF16),
+            pltpu.VMEM((features, places), BF16),
+            pltpu.VMEM((units, places), BF16),
             pltpu.VMEM((2, token_count, places), BF16),
             pltpu.VMEM((2 * chunks, places, CHUNK), BF16),
             pltpu.VMEM((2 * chunks, places, CHUNK), BF16),
@@ -457,10 +492,12 @@
             bytes_accessed=6 * features * units,
             transcendentals=2 * places * units,
         ),
-    )(tokens, out_grad, routes.T, routes, combine_weights, w_gate[0], w_up[0], w_down[0])
-    mixed, tokens_grad, combine, rows, rows_grad, hidden, gate_grad, up_grad = outs
-    gate_wg, up_wg, down_wg = weight_grads(rows, rows_grad, hidden, gate_grad, up_grad)
-    return mixed, tokens_grad, combine[:2].T, gate_wg[None], up_wg[None], down_wg[None]
+    )(tokens, out_grad, routes.T, combine_weights.T, w_gate[0], w_up[0], w_down[0])
+    mixed, tokens_grad, combine, rows_t, rows_grad, hidden_t, gate_grad, up_grad = outs
+    gate_wg, up_wg, down_wg, mixed, tokens_grad, combine = weight_grads(
+        rows_t, rows_grad, hidden_t, gate_grad, up_grad, mixed, tokens_grad, combine
+    )
+    return mixed, tokens_grad, combine.T, gate_wg[None], up_wg[None], down_wg[None]
 
 
 def solution(mesh):

time: 129 us -> 162 us (1.26)
  Pallas kernels: 116 us -> 161 us
  local copies, waits for them, and re-layouts: 11.2 us -> 0 us
    pallas_call x1, Pallas kernels: 109 us -> 151 us  [shards(): pl.pallas_call(functools.partial(layer_kernel, experts, lines), in_specs=...]
    unnamed x18 -> x0, local copies, waits for them, and re-layouts: 9.92 us -> none
    pallas_call x1, Pallas kernels: 7.08 us -> 9.86 us  [weight_grads(): pl.pallas_call(weight_grad_kernel, grid=(features // block,), in_specs=[p...]
where the time goes in v2:
time: 162 us
  Pallas kernels  161 us (99%)
    pallas_call x1, Pallas kernels, shards(): pl.pallas_call(functools.partial(layer_kernel, experts, lines), in_specs=...  151 us
    pallas_call x1, Pallas kernels, weight_grads(): pl.pallas_call(weight_grad_kernel, grid=(features // block,), in_specs=[p...  9.86 us

profile of v2, /device:TPU:0, one launch (start us, length us, event | category | flops | bytes accessed | tf_op | source)
XLA Modules:
  0.0 161.5 jit_solution(797430308095848857)
XLA Ops:
  0.6 151.0 %shard_map.118 = (bf16[128,2048]{1,0:T(8,128)(2,1)}, bf16[128,2048]{1,0:T(8,128)(2,1)}, f32[2,128]{1,0:T(2,128)}, bf16[2048,256]{1,0:T(8,128)(2,1)}, bf16[256,20...) custom-call(bf16[128,2048]{1,0:T(8,128)(2,1)} %tokens_ref.1, ...), custom_call_target="tpu_custom_call" | custom-call | flops 5637144576 | bytes 11010048 | tf_op jit(solution)/shard_map/pallas_call | solution.py:441
  151.7 9.9 %shard_map.119 = (bf16[2048,896]{1,0:T(8,128)(2,1)}, bf16[2048,896]{1,0:T(8,128)(2,1)}, bf16[896,2048]{1,0:T(8,128)(2,1)}, bf16[128,2048]{1,0:T(8,128)(2,1)}, bf...) custom-call(bf16[2048,256]{1,0:T(8,128)(2,1)} %get-tuple-element.20.rows_t_ref, ...), custom_call_target="tpu_custom_call" | custom-call | flops 2818572288 | bytes 14483456 | tf_op jit(solution)/shard_map/pallas_call | solution.py:401

commit v3 on v2

v3 whole, which is shorter than its diff:
```python
import functools

import jax
import jax.numpy as jnp
from jax import lax
from jax.experimental import pallas as pl
from jax.experimental.pallas import tpu as pltpu
from jax.sharding import PartitionSpec as P

MESH = pl.DeviceIdType.MESH
BF16 = jnp.bfloat16
F32 = jnp.float32
CHUNK = 512
LANES = 128
LAG = 2
STEP = 256


def dot(left, right):
    return jnp.dot(left, right, preferred_element_type=F32)


def contract_last(left, right):
    return lax.dot_general(left, right, (((1,), (1,)), ((), ())), preferred_element_type=F32)


def contract_first(left, right):
    return lax.dot_general(left, right, (((0,), (0,)), ((), ())), preferred_element_type=F32)


def one_hot_places(routes_row, routes_col, cap, places):
    tokens = routes_row.shape[1]
    before_by = lax.broadcasted_iota(jnp.int32, (tokens, tokens), 0)
    before_at = lax.broadcasted_iota(jnp.int32, (tokens, tokens), 1)
    upper = (before_by < before_at).astype(F32).astype(BF16)
    lower = (before_by > before_at).astype(F32).astype(BF16)
    expert_down = lax.broadcasted_iota(jnp.int32, (LANES, tokens), 0)
    expert_across = lax.broadcasted_iota(jnp.int32, (tokens, LANES), 1)
    named_down = [(expert_down == routes_row[k : k + 1, :]).astype(F32) for k in range(2)]
    named_across = [
        (expert_across.astype(F32) == routes_col[:, k : k + 1]).astype(F32) for k in range(2)
    ]
    earlier_down = dot((named_down[0] + named_down[1]).astype(BF16), upper)
    earlier_across = dot(lower, (named_across[0] + named_across[1]).astype(BF16))
    start_down = earlier_down + expert_down.astype(F32) * cap
    start_across = earlier_across + expert_across.astype(F32) * cap
    place_down = lax.broadcasted_iota(jnp.int32, (places, tokens), 0).astype(F32)
    place_across = lax.broadcasted_iota(jnp.int32, (tokens, places), 1).astype(F32)
    scatter, gather = [], []
    for k in range(2):
        row = jnp.sum(named_down[k] * start_down, axis=0, keepdims=True)
        col = jnp.sum(named_across[k] * start_across, axis=1, keepdims=True)
        scatter.append((place_down == row).astype(F32).astype(BF16))
        gather.append((place_across == col).astype(F32).astype(BF16))
    return scatter, gather


def layer_kernel(
    experts,
    lines,
    tokens_ref,
    grad_ref,
    routes_ref,
    weights_ref,
    gate_hbm,
    up_hbm,
    down_hbm,
    total_ref,
    combine_ref,
    rows_out,
    hidden_out,
    pre_grad_out,
    both_w,
    down_w,
    send,
    rows,
    pre,
    hidden,
    pre_grad,
    scatter_mat,
    gather_mat,
    weight_cols,
    products,
    part,
    back,
    line_own,
    line_in,
    dot_own,
    dot_in,
    dot_total,
    load_sem,
    store_sem,
    send_sem,
    recv_sem,
    part_sem,
    back_sem,
    inner_sem,
    line_sem,
    outer_sem,
):
    token_count, features = tokens_ref.shape
    cap = token_count // 4
    places = experts * cap
    chunks = features // CHUNK
    last = 2 * chunks
    strips = hidden.shape[1] // LANES
    me = lax.axis_index("expert")
    z = lax.axis_index("etp")
    half = lines // 2
    side = 1 - z // half
    inner = z + 2 * side - 1
    outer = z - 2 * side + 1
    has_outer = jnp.logical_and(z > 0, z < lines - 1)
    center = jnp.logical_or(z == half - 1, z == half)
    kind = jnp.where(center, 1, 0)

    def strip(n, width):
        return pl.ds(pl.multiple_of(n * width, width), width)

    def load(i, n):
        source = (gate_hbm, up_hbm)[i]
        return pltpu.make_async_copy(
            source.at[:, strip(n, LANES)],
            both_w.at[:, strip(2 * n + i, LANES)],
            load_sem.at[2 * n + i],
        )

    def loop(count, start=0):
        return lambda body: lax.fori_loop(start, count, lambda i, c: (body(i), c)[1], 0)

    load_down = pltpu.make_async_copy(down_hbm, down_w, load_sem.at[2 * strips])

    @loop(strips)
    def _(n):
        load(0, n).start()
        load(1, n).start()

    load_down.start()

    barrier = pltpu.get_barrier_semaphore()

    def each_peer(action):
        loop(experts, 1)(lambda d: action(lax.rem(me + d, experts)))

    @each_peer
    def _(peer):
        pl.semaphore_signal(barrier, inc=1, device_id={"expert": peer}, device_id_type=MESH)

    pl.semaphore_signal(barrier, inc=1, device_id={"etp": inner}, device_id_type=MESH)

    @pl.when(has_outer)
    def _():
        pl.semaphore_signal(barrier, inc=1, device_id={"etp": outer}, device_id_type=MESH)

    def block_of(index):
        return strip(index, cap)

    mine = block_of(me)

    def dispatch(i, peer, owner):
        return pltpu.make_async_remote_copy(
            src_ref=send.at[i, block_of(peer)],
            dst_ref=rows.at[i, block_of(owner)],
            send_sem=send_sem.at[i, peer],
            recv_sem=recv_sem.at[i, owner],
            device_id={"expert": peer},
            device_id_type=MESH,
        )

    def give_back(i, peer, owner):
        return pltpu.make_async_remote_copy(
            src_ref=part.at[i, block_of(peer)],
            dst_ref=back.at[i, block_of(owner)],
            send_sem=part_sem.at[i, peer],
            recv_sem=back_sem.at[i, owner],
            device_id={"expert": peer},
            device_id_type=MESH,
        )

    sub = lax.broadcasted_iota(jnp.int32, (LANES, token_count), 0)
    table = jnp.where(sub == 0, routes_ref[0:1, :], routes_ref[1:2, :]).astype(F32)
    table = jnp.where(sub == 2, weights_ref[0:1, :], table)
    table = jnp.where(sub == 3, weights_ref[1:2, :], table).T
    scatter, gather = one_hot_places(routes_ref[...], table, cap, places)
    for k in range(2):
        scatter_mat[k] = scatter[k]
        gather_mat[k] = gather[k]
        weight_cols[k] = jnp.broadcast_to(table[:, 2 + k : 3 + k], (token_count, LANES))
    products[...] = jnp.zeros_like(products)
    scatter_mat[2] = scatter[0] + scatter[1]
    gather_mat[2] = gather[0] + gather[1]

    @loop(features // STEP)
    def _(c):
        cols = strip(c, STEP)
        send[0, :, cols] = dot(scatter_mat[2], tokens_ref[:, cols]).astype(BF16)

    pl.semaphore_wait(barrier, experts + jnp.where(has_outer, 1, 0))
    each_peer(lambda q: dispatch(0, q, me).start())
    rows[0, mine] = send[0, mine]

    @loop(features // STEP)
    def _(c):
        cols = strip(c, STEP)
        value = grad_ref[:, cols].astype(F32)
        scaled = [(weight_cols[k][:, :1] * value).astype(BF16) for k in range(2)]
        send[1, :, cols] = (dot(scatter_mat[0], scaled[0]) + dot(scatter_mat[1], scaled[1])).astype(
            BF16
        )

    each_peer(lambda q: dispatch(1, q, me).start())
    rows[1, mine] = send[1, mine]

    @loop(strips)
    def _(n):
        load(0, n).wait()
        load(1, n).wait()

    load_down.wait()
    each_peer(lambda q: dispatch(0, me, q).wait_recv())

    @loop(strips)
    def _(n):
        both = strip(n, 2 * LANES)
        value = dot(rows[0], both_w[:, both])
        pre[:, both] = value
        gate_value = value[:, :LANES]
        hidden[:, strip(n, LANES)] = (
            gate_value * jax.nn.sigmoid(gate_value) * value[:, LANES:]
        ).astype(BF16)

    def send_back(i):
        each_peer(lambda q: give_back(i, q, me).start())
        back[i, mine] = part[i, mine]

    @loop(chunks)
    def _(c):
        part[c] = dot(hidden[...], down_w[:, strip(c, CHUNK)]).astype(BF16)
        send_back(c)

    each_peer(lambda q: dispatch(1, me, q).wait_recv())

    @loop(strips)
    def _(n):
        both = strip(n, 2 * LANES)
        hidden_grad = contract_last(rows[1], down_w[strip(n, LANES), :])
        value = pre[:, both]
        gate_value, up_value = value[:, :LANES], value[:, LANES:]
        sig = jax.nn.sigmoid(gate_value)
        pre_grad[:, strip(2 * n, LANES)] = (
            hidden_grad * up_value * sig * (1.0 + gate_value * (1.0 - sig))
        ).astype(BF16)
        pre_grad[:, strip(2 * n + 1, LANES)] = (hidden_grad * (gate_value * sig)).astype(BF16)

    stores = [
        pltpu.make_async_copy(src, dst, store_sem.at[i])
        for i, (src, dst) in enumerate(
            ((rows, rows_out), (hidden, hidden_out), (pre_grad, pre_grad_out))
        )
    ]
    for store in stores:
        store.start()

    def line_copy(i, source, where, target, send_line, peer):
        is_dot = isinstance(i, int)
        return pltpu.make_async_remote_copy(
            src_ref=source,
            dst_ref=dot_in.at[where] if is_dot else line_in.at[where, i],
            send_sem=send_line.at[i],
            recv_sem=line_sem.at[target, i],
            device_id={"etp": peer},
            device_id_type=MESH,
        )

    def own_of(i):
        return dot_own if isinstance(i, int) else line_own.at[i]

    def total_of(i):
        return dot_total if isinstance(i, int) else total_ref.at[i]

    def came(i, where):
        return dot_in.at[where] if isinstance(i, int) else line_in.at[where, i]

    def to_inner(i):
        return line_copy(i, own_of(i), kind, kind, inner_sem, inner)

    def to_outer(i):
        return line_copy(i, total_of(i), 1, 1, outer_sem, outer)

    def arrived(i, where):
        return line_copy(i, own_of(i), where, where, inner_sem, inner)

    def inward(i, value):
        own = own_of(i)

        @pl.when(has_outer)
        def _():
            arrived(i, 0).wait_recv()
            own[...] = (value + came(i, 0)[...].astype(F32)).astype(own.dtype)

        @pl.when(jnp.logical_not(has_outer))
        def _():
            own[...] = value.astype(own.dtype)

        to_inner(i).start()

    def outward(i):
        own, total = own_of(i), total_of(i)
        arrived(i, 1).wait_recv()

        @pl.when(center)
        def _():
            total[...] = (own[...].astype(F32) + came(i, 1)[...].astype(F32)).astype(own.dtype)

        @pl.when(jnp.logical_not(center))
        def _():
            total[...] = came(i, 1)[...]

        @pl.when(has_outer)
        def _():
            to_outer(i).start()

    @loop(chunks)
    def _(i):
        j = chunks + i
        cols = strip(i, CHUNK)
        part[j] = contract_last(pre_grad[...], both_w[cols, :]).astype(BF16)
        send_back(j)
        each_peer(lambda q: give_back(i, me, q).wait_recv())
        pairs = [dot(gather_mat[k], back[i]) for k in range(2)]
        value = grad_ref[:, cols].astype(F32)
        for k in range(2):
            term = value * pairs[k]
            products[k] += sum(
                term[:, s * LANES : (s + 1) * LANES] for s in range(CHUNK // LANES)
            )
        inward(i, weight_cols[0][:, :1] * pairs[0] + weight_cols[1][:, :1] * pairs[1])

        @pl.when(i >= LAG)
        def _():
            outward(i - LAG)

    sums = [jnp.sum(products[k], axis=1, keepdims=True) for k in range(2)]
    lane = lax.broadcasted_iota(jnp.int32, (token_count, LANES), 1)
    inward(last, jnp.where(lane == 0, sums[0], jnp.where(lane == 1, sums[1], 0.0)).T[:8])

    @loop(last, chunks)
    def _(j):
        outward(j - LAG)
        each_peer(lambda q: give_back(j, me, q).wait_recv())
        inward(j, dot(gather_mat[2], back[j]))

    outward(last)
    combine_ref[...] = dot_total[:2]
    loop(last, last - LAG)(outward)

    for store in stores:
        store.wait()

    @each_peer
    def _(q):
        dispatch(0, q, me).wait_send()
        dispatch(1, q, me).wait_send()
        loop(last)(lambda i: give_back(i, q, me).wait_send())

    loop(last)(lambda i: to_inner(i).wait_send())
    to_inner(last).wait_send()

    @pl.when(has_outer)
    def _():
        loop(last)(lambda i: to_outer(i).wait_send())
        to_outer(last).wait_send()


def weight_grad_kernel(
    rows_ref,
    rows_grad_ref,
    hidden_ref,
    pre_grad_ref,
    mixed_ref,
    tokens_grad_ref,
    combine_ref,
    gate_out,
    up_out,
    down_out,
    mixed_out,
    tokens_grad_out,
    combine_out,
    hidden_t,
    rows_t,
):
    strips = hidden_ref.shape[1] // LANES

    def strip(n, width):
        return pl.ds(pl.multiple_of(n * width, width), width)

    def turn(n, carry):
        hidden_t[strip(n, LANES), :] = hidden_ref[:, strip(n, LANES)].T
        return carry

    @pl.when(pl.program_id(0) == 0)
    def _():
        lax.fori_loop(0, strips, turn, 0)

    mixed_out[...] = mixed_ref[0]
    tokens_grad_out[...] = tokens_grad_ref[0]
    combine_out[...] = combine_ref[...]
    rows_t[...] = rows_ref[0].T

    def step(n, carry):
        one = strip(n, LANES)
        both = dot(rows_t[...], pre_grad_ref[:, strip(n, 2 * LANES)]).astype(BF16)
        gate_out[:, one] = both[:, :LANES]
        up_out[:, one] = both[:, LANES:]
        down_out[one, :] = dot(hidden_t[one, :], rows_grad_ref[0]).astype(BF16)
        return carry

    lax.fori_loop(0, strips, step, 0)


def weight_grads(rows, hidden, pre_grad, total, combine):
    _, places, features = rows.shape
    units = hidden.shape[1]
    chunks, token_count = total.shape[0] // 2, total.shape[1]
    split = CHUNK // STEP
    tall = pl.BlockSpec((STEP, units), lambda i: (i, 0))
    wide = pl.BlockSpec((units, STEP), lambda i: (0, i))
    token_cols = pl.BlockSpec((token_count, STEP), lambda i: (0, i))
    pair_sums = pl.BlockSpec((2, token_count), lambda i: (0, 0))
    return pl.pallas_call(
        weight_grad_kernel,
        grid=(features // STEP,),
        in_specs=[
            pl.BlockSpec((1, places, STEP), lambda i: (0, 0, i)),
            pl.BlockSpec((1, places, STEP), lambda i: (1, 0, i)),
            pl.BlockSpec((places, units), lambda i: (0, 0)),
            pl.BlockSpec((places, 2 * units), lambda i: (0, 0)),
            pl.BlockSpec((1, token_count, STEP), lambda i: (i // split, 0, i % split)),
            pl.BlockSpec((1, token_count, STEP), lambda i: (chunks + i // split, 0, i % split)),
            pair_sums,
        ],
        out_specs=[tall, tall, wide, token_cols, token_cols, pair_sums],
        out_shape=[
            jax.ShapeDtypeStruct((features, units), BF16),
            jax.ShapeDtypeStruct((features, units), BF16),
            jax.ShapeDtypeStruct((units, features), BF16),
            jax.ShapeDtypeStruct((token_count, features), BF16),
            jax.ShapeDtypeStruct((token_count, features), BF16),
            jax.ShapeDtypeStruct((2, token_count), F32),
        ],
        scratch_shapes=[pltpu.VMEM((units, places), BF16), pltpu.VMEM((STEP, places), BF16)],
        compiler_params=pltpu.CompilerParams(vmem_limit_bytes=60 << 20),
        cost_estimate=pl.CostEstimate(
            flops=6 * places * features * units,
            bytes_accessed=6 * features * units + 4 * places * features + 6 * places * units,
            transcendentals=0,
        ),
    )(rows, rows, hidden, pre_grad, total, total, combine)


def shards(experts, lines, tokens, out_grad, routes, combine_weights, w_gate, w_up, w_down):
    token_count, features = tokens.shape
    units = w_gate.shape[2]
    cap = token_count // 4
    places = experts * cap
    chunks = features // CHUNK
    items = 2 * chunks
    vmem = pl.BlockSpec(memory_space=pltpu.VMEM)
    hbm = pl.BlockSpec(memory_space=pl.ANY)
    dma = pltpu.SemaphoreType.DMA
    total, combine, rows, hidden, pre_grad = pl.pallas_call(
        functools.partial(layer_kernel, experts, lines),
        in_specs=[vmem] * 4 + [hbm] * 3,
        out_specs=[vmem] * 2 + [hbm] * 3,
        out_shape=[
            jax.ShapeDtypeStruct((items, token_count, CHUNK), BF16),
            jax.ShapeDtypeStruct((2, token_count), F32),
            jax.ShapeDtypeStruct((2, places, features), BF16),
            jax.ShapeDtypeStruct((places, units), BF16),
            jax.ShapeDtypeStruct((places, 2 * units), BF16),
        ],
        scratch_shapes=[
            pltpu.VMEM((features, 2 * units), BF16),
            pltpu.VMEM((units, features), BF16),
            pltpu.VMEM((2, places, features), BF16),
            pltpu.VMEM((2, places, features), BF16),
            pltpu.VMEM((places, 2 * units), F32),
            pltpu.VMEM((places, units), BF16),
            pltpu.VMEM((places, 2 * units), BF16),
            pltpu.VMEM((3, places, token_count), BF16),
            pltpu.VMEM((3, token_count, places), BF16),
            pltpu.VMEM((2, token_count, LANES), F32),
            pltpu.VMEM((2, token_count, LANES), F32),
            pltpu.VMEM((items, places, CHUNK), BF16),
            pltpu.VMEM((items, places, CHUNK), BF16),
            pltpu.VMEM((items, token_count, CHUNK), BF16),
            pltpu.VMEM((2, items, token_count, CHUNK), BF16),
            pltpu.VMEM((8, token_count), F32),
            pltpu.VMEM((2, 8, token_count), F32),
            pltpu.VMEM((8, token_count), F32),
            dma((2 * (units // LANES) + 1,)),
            dma((3,)),
            dma((2, experts)),
            dma((2, experts)),
            dma((items, experts)),
            dma((items, experts)),
            dma((items + 1,)),
            dma((2, items + 1)),
            dma((items + 1,)),
        ],
        compiler_params=pltpu.CompilerParams(
            collective_id=0, has_side_effects=True, vmem_limit_bytes=56 << 20
        ),
        cost_estimate=pl.CostEstimate(
            flops=12 * places * features * units,
            bytes_accessed=6 * features * units,
            transcendentals=2 * places * units,
        ),
    )(tokens, out_grad, routes.T, combine_weights.T, w_gate[0], w_up[0], w_down[0])
    gate_wg, up_wg, down_wg, mixed, tokens_grad, combine = weight_grads(
        rows, hidden, pre_grad, total, combine
    )
    return mixed, tokens_grad, combine.T, gate_wg[None], up_wg[None], down_wg[None]


def solution(mesh):
    rows = P("expert", None)
    columns = P("expert", None, "etp")
    return jax.shard_map(
        functools.partial(shards, mesh.shape["expert"], mesh.shape["etp"]),
        mesh=mesh,
        in_specs=(rows, rows, rows, rows, columns, columns, P("expert", "etp", None)),
        out_specs=(rows, rows, rows, columns, columns, P("expert", "etp", None)),
        check_vma=False,
    )
```

time: 162 us -> 129 us (0.80)
  Pallas kernels: 161 us -> 128 us
    pallas_call x1, Pallas kernels: 151 us -> 111 us  [shards(): pl.pallas_call(functools.partial(layer_kernel, experts, lines), in_specs=...]
    pallas_call x1, Pallas kernels: 9.86 us -> 17.3 us  [weight_grads(): pl.pallas_call(weight_grad_kernel, grid=(features // STEP,), in_specs=[pl...]
where the time goes in v3:
time: 129 us
  Pallas kernels  128 us (99%)
    pallas_call x1, Pallas kernels, shards(): pl.pallas_call(functools.partial(layer_kernel, experts, lines), in_specs=...  111 us
    pallas_call x1, Pallas kernels, weight_grads(): pl.pallas_call(weight_grad_kernel, grid=(features // STEP,), in_specs=[pl...  17.3 us

profile of v3, /device:TPU:0, one launch (start us, length us, event | category | flops | bytes accessed | tf_op | source)
XLA Modules:
  0.0 129.1 jit_solution(114964067868880658)
XLA Ops:
  0.6 111.1 %shard_map.118 = (bf16[8,128,512]{2,1,0:T(8,128)(2,1)}, f32[2,128]{1,0:T(2,128)}, bf16[2,256,2048]{2,1,0:T(8,128)(2,1)}, bf16[256,896]{1,0:T(8,128)(2,1)}, bf16[256,1792]{1,0:T(8,128)(2,1)}) custom-call(bf16[128,2048]{1,0:T(8,128)(2,1)} %tokens_ref.1, bf16[128,2048]{1,0:T(8,128)(2,1)} %grad_ref.1, s32[2,128]{1,0:T(2,128)} %bitcast.12, f32[2,128]{1,0:T(2,128)} %bitcast.13, ...), custom_call_target="tpu_custom_call" | custom-call | flops 5637144576 | bytes 11010048 | tf_op jit(solution)/shard_map/pallas_call | solution.py:471
  111.7 17.3 %shard_map.119 = (bf16[2048,896]{1,0:T(8,128)(2,1)}, bf16[2048,896]{1,0:T(8,128)(2,1)}, bf16[896,2048]{1,0:T(8,128)(2,1)}, bf16[128,2048]{1,0:T(8,128)(2,1)}, bf...) custom-call(bf16[2,256,2048]{2,1,0:T(8,128)(2,1)} %get-tuple-element.17.rows_ref.rows_grad_ref, ...), custom_call_target="tpu_custom_call" | custom-call | flops 2818572288 | bytes 14483456 | tf_op jit(solution)/shard_map/pallas_call | solution.py:430

commit v4 on v3

--- a/solution.py
+++ b/solution.py
@@ -10,9 +10,9 @@
 MESH = pl.DeviceIdType.MESH
 BF16 = jnp.bfloat16
 F32 = jnp.float32
-CHUNK = 512
+CHUNK = 1024
 LANES = 128
-LAG = 2
+LAG = 1
 STEP = 256
 
 
@@ -235,7 +235,11 @@
 
     @loop(chunks)
     def _(c):
-        part[c] = dot(hidden[...], down_w[:, strip(c, CHUNK)]).astype(BF16)
+        @loop(CHUNK // STEP)
+        def _(n):
+            cols = strip(c * (CHUNK // STEP) + n, STEP)
+            part[c, :, strip(n, STEP)] = dot(hidden[...], down_w[:, cols]).astype(BF16)
+
         send_back(c)
 
     each_peer(lambda q: dispatch(1, me, q).wait_recv())
@@ -322,10 +326,18 @@
 
     @loop(chunks)
     def _(i):
-        j = chunks + i
+        @loop(CHUNK // STEP)
+        def _(n):
+            rows_of = strip(i * (CHUNK // STEP) + n, STEP)
+            part[chunks + i, :, strip(n, STEP)] = contract_last(
+                pre_grad[...], both_w[rows_of, :]
+            ).astype(BF16)
+
+        send_back(chunks + i)
+
+    @loop(chunks)
+    def _(i):
         cols = strip(i, CHUNK)
-        part[j] = contract_last(pre_grad[...], both_w[cols, :]).astype(BF16)
-        send_back(j)
         each_peer(lambda q: give_back(i, me, q).wait_recv())
         pairs = [dot(gather_mat[k], back[i]) for k in range(2)]
         value = grad_ref[:, cols].astype(F32)
@@ -373,12 +385,10 @@
 
 
 def weight_grad_kernel(
-    rows_ref,
-    rows_grad_ref,
-    hidden_ref,
-    pre_grad_ref,
-    mixed_ref,
-    tokens_grad_ref,
+    rows_hbm,
+    hidden_hbm,
+    pre_grad_hbm,
+    total_hbm,
     combine_ref,
     gate_out,
     up_out,
@@ -386,60 +396,110 @@
     mixed_out,
     tokens_grad_out,
     combine_out,
+    rows,
+    hidden,
+    pre_grad,
     hidden_t,
-    rows_t,
+    gate_buf,
+    up_buf,
+    down_buf,
+    load_sem,
+    rows_sem,
+    total_sem,
+    store_sem,
 ):
-    strips = hidden_ref.shape[1] // LANES
+    strips = hidden.shape[1] // LANES
+    blocks = rows.shape[2] // STEP
+    chunks = total_hbm.shape[0] // 2
 
     def strip(n, width):
         return pl.ds(pl.multiple_of(n * width, width), width)
 
-    def turn(n, carry):
-        hidden_t[strip(n, LANES), :] = hidden_ref[:, strip(n, LANES)].T
+    def load_rows(k, i):
+        cols = strip(i, STEP)
+        return pltpu.make_async_copy(
+            rows_hbm.at[k, :, cols], rows.at[k, :, cols], rows_sem.at[k, i]
+        )
+
+    def store(i):
+        cols = strip(i, STEP)
+        pairs = (
+            (gate_buf.at[cols, :], gate_out.at[cols, :]),
+            (up_buf.at[cols, :], up_out.at[cols, :]),
+            (down_buf.at[:, cols], down_out.at[:, cols]),
+        )
+        return [
+            pltpu.make_async_copy(src, dst, store_sem.at[k, i])
+            for k, (src, dst) in enumerate(pairs)
+        ]
+
+    loads = [
+        pltpu.make_async_copy(hidden_hbm, hidden, load_sem.at[0]),
+        pltpu.make_async_copy(pre_grad_hbm, pre_grad, load_sem.at[1]),
+    ]
+    for load in loads:
+        load.start()
+
+    def start_rows(i, carry):
+        load_rows(0, i).start()
+        load_rows(1, i).start()
         return carry
 
-    @pl.when(pl.program_id(0) == 0)
-    def _():
-        lax.fori_loop(0, strips, turn, 0)
-
-    mixed_out[...] = mixed_ref[0]
-    tokens_grad_out[...] = tokens_grad_ref[0]
+    lax.fori_loop(0, blocks, start_rows, 0)
+    moves = [
+        pltpu.make_async_copy(
+            total_hbm.at[k * chunks + c],
+            out.at[:, c * CHUNK : (c + 1) * CHUNK],
+            total_sem.at[k * chunks + c],
+        )
+        for k, out in enumerate((mixed_out, tokens_grad_out))
+        for c in range(chunks)
+    ]
+    for move in moves:
+        move.start()
     combine_out[...] = combine_ref[...]
-    rows_t[...] = rows_ref[0].T
-
-    def step(n, carry):
-        one = strip(n, LANES)
-        both = dot(rows_t[...], pre_grad_ref[:, strip(n, 2 * LANES)]).astype(BF16)
-        gate_out[:, one] = both[:, :LANES]
-        up_out[:, one] = both[:, LANES:]
-        down_out[one, :] = dot(hidden_t[one, :], rows_grad_ref[0]).astype(BF16)
+    for load in loads:
+        load.wait()
+    hidden_t[...] = hidden[...].T
+
+    def step(i, carry):
+        cols = strip(i, STEP)
+        load_rows(0, i).wait()
+        load_rows(1, i).wait()
+        both = dot(rows[0, :, cols].T, pre_grad[...]).astype(BF16)
+        for n in range(strips):
+            one = slice(n * LANES, (n + 1) * LANES)
+            gate_buf[cols, one] = both[:, 2 * n * LANES : (2 * n + 1) * LANES]
+            up_buf[cols, one] = both[:, (2 * n + 1) * LANES : (2 * n + 2) * LANES]
+        down_buf[:, cols] = dot(hidden_t[...], rows[1, :, cols]).astype(BF16)
+        for copy in store(i):
+            copy.start()
         return carry
 
-    lax.fori_loop(0, strips, step, 0)
+    lax.fori_loop(0, blocks, step, 0)
+
+    def finish(i, carry):
+        for copy in store(i):
+            copy.wait()
+        return carry
+
+    lax.fori_loop(0, blocks, finish, 0)
+    for move in moves:
+        move.wait()
 
 
 def weight_grads(rows, hidden, pre_grad, total, combine):
     _, places, features = rows.shape
     units = hidden.shape[1]
-    chunks, token_count = total.shape[0] // 2, total.shape[1]
-    split = CHUNK // STEP
-    tall = pl.BlockSpec((STEP, units), lambda i: (i, 0))
-    wide = pl.BlockSpec((units, STEP), lambda i: (0, i))
-    token_cols = pl.BlockSpec((token_count, STEP), lambda i: (0, i))
-    pair_sums = pl.BlockSpec((2, token_count), lambda i: (0, 0))
+    items, token_count, _ = total.shape
+    blocks = features // STEP
+    vmem = pl.BlockSpec(memory_space=pltpu.VMEM)
+    hbm = pl.BlockSpec(memory_space=pl.ANY)
+    dma = pltpu.SemaphoreType.DMA
     return pl.pallas_call(
         weight_grad_kernel,
-        grid=(features // STEP,),
-        in_specs=[
-            pl.BlockSpec((1, places, STEP), lambda i: (0, 0, i)),
-            pl.BlockSpec((1, places, STEP), lambda i: (1, 0, i)),
-            pl.BlockSpec((places, units), lambda i: (0, 0)),
-            pl.BlockSpec((places, 2 * units), lambda i: (0, 0)),
-            pl.BlockSpec((1, token_count, STEP), lambda i: (i // split, 0, i % split)),
-            pl.BlockSpec((1, token_count, STEP), lambda i: (chunks + i // split, 0, i % split)),
-            pair_sums,
-        ],
-        out_specs=[tall, tall, wide, token_cols, token_cols, pair_sums],
+        in_specs=[hbm] * 4 + [vmem],
+        out_specs=[hbm] * 5 + [vmem],
         out_shape=[
             jax.ShapeDtypeStruct((features, units), BF16),
             jax.ShapeDtypeStruct((features, units), BF16),
@@ -448,14 +508,26 @@
             jax.ShapeDtypeStruct((token_count, features), BF16),
             jax.ShapeDtypeStruct((2, token_count), F32),
         ],
-        scratch_shapes=[pltpu.VMEM((units, places), BF16), pltpu.VMEM((STEP, places), BF16)],
+        scratch_shapes=[
+            pltpu.VMEM((2, places, features), BF16),
+            pltpu.VMEM((places, units), BF16),
+            pltpu.VMEM((places, 2 * units), BF16),
+            pltpu.VMEM((units, places), BF16),
+            pltpu.VMEM((features, units), BF16),
+            pltpu.VMEM((features, units), BF16),
+            pltpu.VMEM((units, features), BF16),
+            dma((2,)),
+            dma((2, blocks)),
+            dma((items,)),
+            dma((3, blocks)),
+        ],
         compiler_params=pltpu.CompilerParams(vmem_limit_bytes=60 << 20),
         cost_estimate=pl.CostEstimate(
             flops=6 * places * features * units,
             bytes_accessed=6 * features * units + 4 * places * features + 6 * places * units,
             transcendentals=0,
         ),
-    )(rows, rows, hidden, pre_grad, total, total, combine)
+    )(rows, hidden, pre_grad, total, combine)
 
 
 def shards(experts, lines, tokens, out_grad, routes, combine_weights, w_gate, w_up, w_down):

time: 129 us -> 142 us (1.10)
  Pallas kernels: 128 us -> 141 us
    pallas_call x1, Pallas kernels: 17.3 us -> 34.5 us  [weight_grads(): pl.pallas_call(weight_grad_kernel, in_specs=[hbm] * 4 + [vmem], out_specs...]
    pallas_call x1, Pallas kernels: 111 us -> 106 us  [shards(): pl.pallas_call(functools.partial(layer_kernel, experts, lines), in_specs=...]
where the time goes in v4:
time: 142 us
  Pallas kernels  141 us (99%)
    pallas_call x1, Pallas kernels, shards(): pl.pallas_call(functools.partial(layer_kernel, experts, lines), in_specs=...  106 us
    pallas_call x1, Pallas kernels, weight_grads(): pl.pallas_call(weight_grad_kernel, in_specs=[hbm] * 4 + [vmem], out_specs...  34.5 us

profile of v4, /device:TPU:0, one launch (start us, length us, event | category | flops | bytes accessed | tf_op | source)
XLA Modules:
  0.0 141.6 jit_solution(9448982752827853972)
XLA Ops:
  0.6 106.4 %shard_map.118 = (bf16[4,128,1024]{2,1,0:T(8,128)(2,1)}, f32[2,128]{1,0:T(2,128)}, bf16[2,256,2048]{2,1,0:T(8,128)(2,1)}, bf16[256,896]{1,0:T(8,128)(2,1)}, bf16[256,1792]{1,0:T(8,128)(2,1)}) custom-call(bf16[128,2048]{1,0:T(8,128)(2,1)} %tokens_ref.1, bf16[128,2048]{1,0:T(8,128)(2,1)} %grad_ref.1, s32[2,128]{1,0:T(2,128)} %bitcast.12, f32[2,128]{1,0:T(2,128)} %bitcast.13, ...), custom_call_target="tpu_custom_call" | custom-call | flops 5637144576 | bytes 11010048 | tf_op jit(solution)/shard_map/pallas_call | solution.py:543
  107.1 34.5 %shard_map.119 = (bf16[2048,896]{1,0:T(8,128)(2,1)}, bf16[2048,896]{1,0:T(8,128)(2,1)}, bf16[896,2048]{1,0:T(8,128)(2,1)}, bf16[128,2048]{1,0:T(8,128)(2,1)}, bf...) custom-call(bf16[2,256,2048]{2,1,0:T(8,128)(2,1)} %get-tuple-element.17.rows_hbm, ...), custom_call_target="tpu_custom_call" | custom-call | flops 2818572288 | bytes 14483456 | tf_op jit(solution)/shard_map/pallas_call | solution.py:499

commit v5 on v3

--- a/solution.py
+++ b/solution.py
@@ -10,9 +10,11 @@
 MESH = pl.DeviceIdType.MESH
 BF16 = jnp.bfloat16
 F32 = jnp.float32
-CHUNK = 512
+CHUNK = 1024
 LANES = 128
 LAG = 2
+LINE = 512
+SHARED = 3 / 8
 STEP = 256
 
 
@@ -92,6 +94,8 @@
     store_sem,
     send_sem,
     recv_sem,
+    pass_send_sem,
+    pass_recv_sem,
     part_sem,
     back_sem,
     inner_sem,
@@ -102,7 +106,11 @@
     cap = token_count // 4
     places = experts * cap
     chunks = features // CHUNK
-    last = 2 * chunks
+    items = 2 * chunks
+    split = CHUNK // LINE
+    last = items * split
+    shared = int(features * SHARED) // LANES * LANES
+    kept = features - shared
     strips = hidden.shape[1] // LANES
     me = lax.axis_index("expert")
     z = lax.axis_index("etp")
@@ -113,6 +121,8 @@
     has_outer = jnp.logical_and(z > 0, z < lines - 1)
     center = jnp.logical_or(z == half - 1, z == half)
     kind = jnp.where(center, 1, 0)
+    parity = lax.rem(z, 2)
+    partner = z + 1 - 2 * parity
 
     def strip(n, width):
         return pl.ds(pl.multiple_of(n * width, width), width)
@@ -158,14 +168,37 @@
     mine = block_of(me)
 
     def dispatch(i, peer, owner):
+        cols = pl.ds(pl.multiple_of(parity * shared, LANES), kept)
         return pltpu.make_async_remote_copy(
-            src_ref=send.at[i, block_of(peer)],
-            dst_ref=rows.at[i, block_of(owner)],
+            src_ref=send.at[i, block_of(peer), cols],
+            dst_ref=rows.at[i, block_of(owner), cols],
             send_sem=send_sem.at[i, peer],
             recv_sem=recv_sem.at[i, owner],
             device_id={"expert": peer},
             device_id_type=MESH,
         )
+
+    def pass_on(i, owner, side_of):
+        cols = pl.ds(pl.multiple_of(side_of * kept, LANES), shared)
+        return pltpu.make_async_remote_copy(
+            src_ref=rows.at[i, block_of(owner), cols],
+            dst_ref=rows.at[i, block_of(owner), cols],
+            send_sem=pass_send_sem.at[i, owner],
+            recv_sem=pass_recv_sem.at[i, owner],
+            device_id={"etp": partner},
+            device_id_type=MESH,
+        )
+
+    def receive(i):
+        def one(d):
+            q = lax.rem(me + experts - d, experts)
+            dispatch(i, me, q).wait_recv()
+            pass_on(i, q, parity).start()
+
+        loop(experts, 1)(one)
+
+    def passed(i):
+        each_peer(lambda q: pass_on(i, q, 1 - parity).wait_recv())
 
     def give_back(i, peer, owner):
         return pltpu.make_async_remote_copy(
@@ -217,7 +250,8 @@
         load(1, n).wait()
 
     load_down.wait()
-    each_peer(lambda q: dispatch(0, me, q).wait_recv())
+    receive(0)
+    passed(0)
 
     @loop(strips)
     def _(n):
@@ -229,16 +263,22 @@
             gate_value * jax.nn.sigmoid(gate_value) * value[:, LANES:]
         ).astype(BF16)
 
+    receive(1)
+
     def send_back(i):
         each_peer(lambda q: give_back(i, q, me).start())
         back[i, mine] = part[i, mine]
 
     @loop(chunks)
     def _(c):
-        part[c] = dot(hidden[...], down_w[:, strip(c, CHUNK)]).astype(BF16)
+        @loop(CHUNK // STEP)
+        def _(n):
+            cols = strip(c * (CHUNK // STEP) + n, STEP)
+            part[c, :, strip(n, STEP)] = dot(hidden[...], down_w[:, cols]).astype(BF16)
+
         send_back(c)
 
-    each_peer(lambda q: dispatch(1, me, q).wait_recv())
+    passed(1)
 
     @loop(strips)
     def _(n):
@@ -322,33 +362,48 @@
 
     @loop(chunks)
     def _(i):
-        j = chunks + i
-        cols = strip(i, CHUNK)
-        part[j] = contract_last(pre_grad[...], both_w[cols, :]).astype(BF16)
-        send_back(j)
+        @loop(CHUNK // STEP)
+        def _(n):
+            rows_of = strip(i * (CHUNK // STEP) + n, STEP)
+            part[chunks + i, :, strip(n, STEP)] = contract_last(
+                pre_grad[...], both_w[rows_of, :]
+            ).astype(BF16)
+
+        send_back(chunks + i)
+
+    @loop(chunks)
+    def _(i):
         each_peer(lambda q: give_back(i, me, q).wait_recv())
-        pairs = [dot(gather_mat[k], back[i]) for k in range(2)]
-        value = grad_ref[:, cols].astype(F32)
-        for k in range(2):
-            term = value * pairs[k]
-            products[k] += sum(
-                term[:, s * LANES : (s + 1) * LANES] for s in range(CHUNK // LANES)
-            )
-        inward(i, weight_cols[0][:, :1] * pairs[0] + weight_cols[1][:, :1] * pairs[1])
-
-        @pl.when(i >= LAG)
-        def _():
-            outward(i - LAG)
+
+        @loop(split)
+        def _(n):
+            at = i * split + n
+            pairs = [dot(gather_mat[k], back[i, :, strip(n, LINE)]) for k in range(2)]
+            value = grad_ref[:, strip(at, LINE)].astype(F32)
+            for k in range(2):
+                term = value * pairs[k]
+                products[k] += sum(
+                    term[:, s * LANES : (s + 1) * LANES] for s in range(LINE // LANES)
+                )
+            inward(at, weight_cols[0][:, :1] * pairs[0] + weight_cols[1][:, :1] * pairs[1])
+
+            @pl.when(at >= LAG)
+            def _():
+                outward(at - LAG)
 
     sums = [jnp.sum(products[k], axis=1, keepdims=True) for k in range(2)]
     lane = lax.broadcasted_iota(jnp.int32, (token_count, LANES), 1)
     inward(last, jnp.where(lane == 0, sums[0], jnp.where(lane == 1, sums[1], 0.0)).T[:8])
 
-    @loop(last, chunks)
+    @loop(items, chunks)
     def _(j):
-        outward(j - LAG)
         each_peer(lambda q: give_back(j, me, q).wait_recv())
-        inward(j, dot(gather_mat[2], back[j]))
+
+        @loop(split)
+        def _(n):
+            at = j * split + n
+            outward(at - LAG)
+            inward(at, dot(gather_mat[2], back[j, :, strip(n, LINE)]))
 
     outward(last)
     combine_ref[...] = dot_total[:2]
@@ -361,7 +416,9 @@
     def _(q):
         dispatch(0, q, me).wait_send()
         dispatch(1, q, me).wait_send()
-        loop(last)(lambda i: give_back(i, q, me).wait_send())
+        pass_on(0, q, parity).wait_send()
+        pass_on(1, q, parity).wait_send()
+        loop(items)(lambda i: give_back(i, q, me).wait_send())
 
     loop(last)(lambda i: to_inner(i).wait_send())
     to_inner(last).wait_send()
@@ -407,22 +464,19 @@
     combine_out[...] = combine_ref[...]
     rows_t[...] = rows_ref[0].T
 
-    def step(n, carry):
-        one = strip(n, LANES)
-        both = dot(rows_t[...], pre_grad_ref[:, strip(n, 2 * LANES)]).astype(BF16)
-        gate_out[:, one] = both[:, :LANES]
-        up_out[:, one] = both[:, LANES:]
-        down_out[one, :] = dot(hidden_t[one, :], rows_grad_ref[0]).astype(BF16)
-        return carry
-
-    lax.fori_loop(0, strips, step, 0)
+    both = dot(rows_t[...], pre_grad_ref[...]).astype(BF16)
+    for n in range(strips):
+        one = slice(n * LANES, (n + 1) * LANES)
+        gate_out[:, one] = both[:, 2 * n * LANES : (2 * n + 1) * LANES]
+        up_out[:, one] = both[:, (2 * n + 1) * LANES : (2 * n + 2) * LANES]
+    down_out[...] = dot(hidden_t[...], rows_grad_ref[0]).astype(BF16)
 
 
 def weight_grads(rows, hidden, pre_grad, total, combine):
     _, places, features = rows.shape
     units = hidden.shape[1]
     chunks, token_count = total.shape[0] // 2, total.shape[1]
-    split = CHUNK // STEP
+    split = LINE // STEP
     tall = pl.BlockSpec((STEP, units), lambda i: (i, 0))
     wide = pl.BlockSpec((units, STEP), lambda i: (0, i))
     token_cols = pl.BlockSpec((token_count, STEP), lambda i: (0, i))
@@ -465,6 +519,7 @@
     places = experts * cap
     chunks = features // CHUNK
     items = 2 * chunks
+    line_items = items * CHUNK // LINE
     vmem = pl.BlockSpec(memory_space=pltpu.VMEM)
     hbm = pl.BlockSpec(memory_space=pl.ANY)
     dma = pltpu.SemaphoreType.DMA
@@ -473,7 +528,7 @@
         in_specs=[vmem] * 4 + [hbm] * 3,
         out_specs=[vmem] * 2 + [hbm] * 3,
         out_shape=[
-            jax.ShapeDtypeStruct((items, token_count, CHUNK), BF16),
+            jax.ShapeDtypeStruct((line_items, token_count, LINE), BF16),
             jax.ShapeDtypeStruct((2, token_count), F32),
             jax.ShapeDtypeStruct((2, places, features), BF16),
             jax.ShapeDtypeStruct((places, units), BF16),
@@ -493,8 +548,8 @@
             pltpu.VMEM((2, token_count, LANES), F32),
             pltpu.VMEM((items, places, CHUNK), BF16),
             pltpu.VMEM((items, places, CHUNK), BF16),
-            pltpu.VMEM((items, token_count, CHUNK), BF16),
-            pltpu.VMEM((2, items, token_count, CHUNK), BF16),
+            pltpu.VMEM((line_items, token_count, LINE), BF16),
+            pltpu.VMEM((2, line_items, token_count, LINE), BF16),
             pltpu.VMEM((8, token_count), F32),
             pltpu.VMEM((2, 8, token_count), F32),
             pltpu.VMEM((8, token_count), F32),
@@ -502,11 +557,13 @@
             dma((3,)),
             dma((2, experts)),
             dma((2, experts)),
+            dma((2, experts)),
+            dma((2, experts)),
             dma((items, experts)),
             dma((items, experts)),
-            dma((items + 1,)),
-            dma((2, items + 1)),
-            dma((items + 1,)),
+            dma((line_items + 1,)),
+            dma((2, line_items + 1)),
+            dma((line_items + 1,)),
         ],
         compiler_params=pltpu.CompilerParams(
             collective_id=0, has_side_effects=True, vmem_limit_bytes=56 << 20

time: 129 us -> 125 us (0.969)
  Pallas kernels: 128 us -> 124 us
    pallas_call x1, Pallas kernels: 17.3 us -> 10.4 us  [weight_grads(): pl.pallas_call(weight_grad_kernel, grid=(features // STEP,), in_specs=[pl...]
    pallas_call x1, Pallas kernels: 111 us -> 113 us  [shards(): pl.pallas_call(functools.partial(layer_kernel, experts, lines), in_specs=...]
where the time goes in v5:
time: 125 us; the launch traced here: 124 us
  Pallas kernels  124 us (99%)
    pallas_call x1, Pallas kernels, shards(): pl.pallas_call(functools.partial(layer_kernel, experts, lines), in_specs=...  113 us
    pallas_call x1, Pallas kernels, weight_grads(): pl.pallas_call(weight_grad_kernel, grid=(features // STEP,), in_specs=[pl...  10.4 us

profile of v5, /device:TPU:0, one launch (start us, length us, event | category | flops | bytes accessed | tf_op | source)
XLA Modules:
  0.0 124.2 jit_solution(18362758008244089608)
XLA Ops:
  0.6 113.2 %shard_map.118 = (bf16[8,128,512]{2,1,0:T(8,128)(2,1)}, f32[2,128]{1,0:T(2,128)}, bf16[2,256,2048]{2,1,0:T(8,128)(2,1)}, bf16[256,896]{1,0:T(8,128)(2,1)}, bf16[256,1792]{1,0:T(8,128)(2,1)}) custom-call(bf16[128,2048]{1,0:T(8,128)(2,1)} %tokens_ref.1, bf16[128,2048]{1,0:T(8,128)(2,1)} %grad_ref.1, s32[2,128]{1,0:T(2,128)} %bitcast.12, f32[2,128]{1,0:T(2,128)} %bitcast.13, ...), custom_call_target="tpu_custom_call" | custom-call | flops 5637144576 | bytes 11010048 | tf_op jit(solution)/shard_map/pallas_call | solution.py:526
  113.8 10.4 %shard_map.119 = (bf16[2048,896]{1,0:T(8,128)(2,1)}, bf16[2048,896]{1,0:T(8,128)(2,1)}, bf16[896,2048]{1,0:T(8,128)(2,1)}, bf16[128,2048]{1,0:T(8,128)(2,1)}, bf...) custom-call(bf16[2,256,2048]{2,1,0:T(8,128)(2,1)} %get-tuple-element.17.rows_ref.rows_grad_ref, ...), custom_call_target="tpu_custom_call" | custom-call | flops 2818572288 | bytes 14483456 | tf_op jit(solution)/shard_map/pallas_call | solution.py:484

commit v6 on v5

--- a/solution.py
+++ b/solution.py
@@ -12,7 +12,7 @@
 F32 = jnp.float32
 CHUNK = 1024
 LANES = 128
-LAG = 2
+LAG = 3
 LINE = 512
 SHARED = 3 / 8
 STEP = 256
@@ -387,7 +387,7 @@
                 )
             inward(at, weight_cols[0][:, :1] * pairs[0] + weight_cols[1][:, :1] * pairs[1])
 
-            @pl.when(at >= LAG)
+            @pl.when(jnp.logical_and(center, at >= LAG))
             def _():
                 outward(at - LAG)
 
@@ -402,12 +402,16 @@
         @loop(split)
         def _(n):
             at = j * split + n
-            outward(at - LAG)
+
+            @pl.when(center)
+            def _():
+                outward(at - LAG)
+
             inward(at, dot(gather_mat[2], back[j, :, strip(n, LINE)]))
 
+    loop(last, jnp.where(center, last - LAG, 0))(outward)
     outward(last)
     combine_ref[...] = dot_total[:2]
-    loop(last, last - LAG)(outward)
 
     for store in stores:
         store.wait()

time: 125 us -> 90.1 us (0.72)
  Pallas kernels: 124 us -> 89.1 us
    pallas_call x1, Pallas kernels: 113 us -> 78.7 us  [shards(): pl.pallas_call(functools.partial(layer_kernel, experts, lines), in_specs=...]
where the time goes in v6:
time: 90.1 us; the launch traced here: 89.7 us
  Pallas kernels  89.1 us (99%)
    pallas_call x1, Pallas kernels, shards(): pl.pallas_call(functools.partial(layer_kernel, experts, lines), in_specs=...  78.7 us
    pallas_call x1, Pallas kernels, weight_grads(): pl.pallas_call(weight_grad_kernel, grid=(features // STEP,), in_specs=[pl...  10.4 us

profile of v6, /device:TPU:0, one launch (start us, length us, event | category | flops | bytes accessed | tf_op | source)
XLA Modules:
  0.0 89.7 jit_solution(5486232083852269149)
XLA Ops:
  0.6 78.7 %shard_map.118 = (bf16[8,128,512]{2,1,0:T(8,128)(2,1)}, f32[2,128]{1,0:T(2,128)}, bf16[2,256,2048]{2,1,0:T(8,128)(2,1)}, bf16[256,896]{1,0:T(8,128)(2,1)}, bf16[256,1792]{1,0:T(8,128)(2,1)}) custom-call(bf16[128,2048]{1,0:T(8,128)(2,1)} %tokens_ref.1, bf16[128,2048]{1,0:T(8,128)(2,1)} %grad_ref.1, s32[2,128]{1,0:T(2,128)} %bitcast.12, f32[2,128]{1,0:T(2,128)} %bitcast.13, ...), custom_call_target="tpu_custom_call" | custom-call | flops 5637144576 | bytes 11010048 | tf_op jit(solution)/shard_map/pallas_call | solution.py:530
  79.3 10.4 %shard_map.119 = (bf16[2048,896]{1,0:T(8,128)(2,1)}, bf16[2048,896]{1,0:T(8,128)(2,1)}, bf16[896,2048]{1,0:T(8,128)(2,1)}, bf16[128,2048]{1,0:T(8,128)(2,1)}, bf...) custom-call(bf16[2,256,2048]{2,1,0:T(8,128)(2,1)} %get-tuple-element.17.rows_ref.rows_grad_ref, ...), custom_call_target="tpu_custom_call" | custom-call | flops 2818572288 | bytes 14483456 | tf_op jit(solution)/shard_map/pallas_call | solution.py:488

commit v7 on v6

--- a/solution.py
+++ b/solution.py
@@ -10,7 +10,7 @@
 MESH = pl.DeviceIdType.MESH
 BF16 = jnp.bfloat16
 F32 = jnp.float32
-CHUNK = 1024
+CHUNK = 512
 LANES = 128
 LAG = 3
 LINE = 512
@@ -263,8 +263,6 @@
             gate_value * jax.nn.sigmoid(gate_value) * value[:, LANES:]
         ).astype(BF16)
 
-    receive(1)
-
     def send_back(i):
         each_peer(lambda q: give_back(i, q, me).start())
         back[i, mine] = part[i, mine]
@@ -278,6 +276,7 @@
 
         send_back(c)
 
+    receive(1)
     passed(1)
 
     @loop(strips)

time: 90.1 us -> 94.1 us (1.044)
  Pallas kernels: 89.1 us -> 93.2 us
    pallas_call x1, Pallas kernels: 78.7 us -> 82.7 us  [shards(): pl.pallas_call(functools.partial(layer_kernel, experts, lines), in_specs=...]
where the time goes in v7:
time: 94.1 us; the launch traced here: 93.8 us
  Pallas kernels  93.2 us (99%)
    pallas_call x1, Pallas kernels, shards(): pl.pallas_call(functools.partial(layer_kernel, experts, lines), in_specs=...  82.7 us
    pallas_call x1, Pallas kernels, weight_grads(): pl.pallas_call(weight_grad_kernel, grid=(features // STEP,), in_specs=[pl...  10.4 us

profile of v7, /device:TPU:0, one launch (start us, length us, event | category | flops | bytes accessed | tf_op | source)
XLA Modules:
  0.0 93.8 jit_solution(793983801801155912)
XLA Ops:
  0.6 82.7 %shard_map.118 = (bf16[8,128,512]{2,1,0:T(8,128)(2,1)}, f32[2,128]{1,0:T(2,128)}, bf16[2,256,2048]{2,1,0:T(8,128)(2,1)}, bf16[256,896]{1,0:T(8,128)(2,1)}, bf16[256,1792]{1,0:T(8,128)(2,1)}) custom-call(bf16[128,2048]{1,0:T(8,128)(2,1)} %tokens_ref.1, bf16[128,2048]{1,0:T(8,128)(2,1)} %grad_ref.1, s32[2,128]{1,0:T(2,128)} %bitcast.12, f32[2,128]{1,0:T(2,128)} %bitcast.13, ...), custom_call_target="tpu_custom_call" | custom-call | flops 5637144576 | bytes 11010048 | tf_op jit(solution)/shard_map/pallas_call | solution.py:529
  83.4 10.4 %shard_map.119 = (bf16[2048,896]{1,0:T(8,128)(2,1)}, bf16[2048,896]{1,0:T(8,128)(2,1)}, bf16[896,2048]{1,0:T(8,128)(2,1)}, bf16[128,2048]{1,0:T(8,128)(2,1)}, bf...) custom-call(bf16[2,256,2048]{2,1,0:T(8,128)(2,1)} %get-tuple-element.17.rows_ref.rows_grad_ref, ...), custom_call_target="tpu_custom_call" | custom-call | flops 2818572288 | bytes 14483456 | tf_op jit(solution)/shard_map/pallas_call | solution.py:487
